TPU v7x, 32 devices: a whole 2x2x4 slice. The times are simulated.
32 devices in a mesh: dp: 8 (over z, y), tensor: 4 (over x, core).
Axes of the slice: x: 2, y: 2, z: 4, core: 2. Of those that a mesh axis runs over, the one named last changes fastest.
Arguments:
- inputs: bfloat16 [8192, 1024], P('dp'), may hold values from -6 to 6
- memory: bfloat16 [8192, 1024], P('dp'), may hold values from -6 to 6
- prefix: int32 [8], P('dp'), may hold values from 102 to 512, as said below
- self_qkv: bfloat16 [3, 1024, 1024], P(None, None, 'tensor'), may hold values from -0.1875 to 0.1875
- self_bias: bfloat16 [2, 1024], P(None, 'tensor'), may hold values from -3 to 3
- self_out: bfloat16 [1024, 1024], P('tensor'), may hold values from -3 to 3
- cross_qkv: bfloat16 [3, 1024, 1024], P(None, None, 'tensor'), may hold values from -0.1875 to 0.1875
- cross_bias: bfloat16 [2, 1024], P(None, 'tensor'), may hold values from -3 to 3
- cross_out: bfloat16 [1024, 1024], P('tensor'), may hold values from -3 to 3
- ffn_in: bfloat16 [1024, 4096], P(None, 'tensor'), may hold values from -0.1875 to 0.1875
- ffn_in_bias: bfloat16 [4096], P('tensor'), may hold values from -3 to 3
- ffn_out: bfloat16 [4096, 1024], P('tensor'), may hold values from -0.09375 to 0.09375
- norm_gain: bfloat16 [1024, 3], replicated, may hold values from 0.5 to 1.5
- norm_shift: bfloat16 [1024, 3], replicated, may hold values from -2 to 2
- out_bias: bfloat16 [1024, 3], replicated, may hold values from -2 to 2
- cotangent: bfloat16 [8192, 1024], P(('dp', 'tensor')), may hold values from -6 to 6
Outputs:
- output: bfloat16 [8192, 1024], P(('dp', 'tensor'))
- input_grad: bfloat16 [8192, 1024], P(('dp', 'tensor'))
- memory_grad: bfloat16 [8192, 1024], P(('dp', 'tensor'))
- self_qkv_grad: float32 [3, 1024, 1024], P(None, None, 'tensor')
- self_bias_grad: float32 [2, 1024], P(None, 'tensor')
- self_out_grad: float32 [1024, 1024], P('tensor')
- cross_qkv_grad: float32 [3, 1024, 1024], P(None, None, 'tensor')
- cross_bias_grad: float32 [2, 1024], P(None, 'tensor')
- cross_out_grad: float32 [1024, 1024], P('tensor')
- ffn_in_grad: float32 [1024, 4096], P(None, 'tensor')
- ffn_in_bias_grad: float32 [4096], P('tensor')
- ffn_out_grad: float32 [4096, 1024], P('tensor')
- norm_gain_grad: float32 [1024, 3], P('tensor')
- norm_shift_grad: float32 [1024, 3], P('tensor')
- out_bias_grad: float32 [1024, 3], P('tensor')
Inputs may be any that keep to these rules, and one draw needn't show every extreme that they name: prefix[s] is the number of leading positions of sequence s whose tokens see each other both ways; some sequence has exactly 102 and some exactly 512.
All inputs are finite; a program needn't handle non-finite values.
Results may differ from a plain program's by a relative error of at most 0.024.
The roundings to bfloat16 on the way count: a program that leaves them out, or rounds other values in their place, can miss the bound.
Values may be sent and summed in bfloat16 or wider, within the bound.
A program may use at most 192 MiB of HBM per device.

v0:
```python
import math

import jax
import jax.numpy as jnp
from jax import lax
from jax.sharding import PartitionSpec as P

HEAD_DIM = 64


epsilon = 1e-05
masked_score = -1e30


def norm_forward(values, gains, shifts):
    centered = values - jnp.mean(values, axis=-1, keepdims=True)
    inverse = lax.rsqrt(jnp.mean(centered * centered, axis=-1, keepdims=True) + epsilon)
    normed = centered * inverse
    return (normed * gains + shifts, normed, inverse)


def norm_backward(upstream, normed, inverse, gains):
    scaled = upstream * gains
    into = inverse * (
        scaled
        - jnp.mean(scaled, axis=-1, keepdims=True)
        - normed * jnp.mean(scaled * normed, axis=-1, keepdims=True)
    )
    return (into, jnp.sum(upstream * normed, axis=0), jnp.sum(upstream, axis=0))


def rows_product(lhs_rows, rhs_rows):
    return lax.dot_general(
        lhs_rows, rhs_rows, (((0,), (0,)), ((), ())), preferred_element_type=jnp.float32
    )


def times_transpose(lhs_rows, weight):
    return lax.dot_general(
        lhs_rows, weight, (((1,), (1,)), ((), ())), preferred_element_type=jnp.float32
    )


def forward_term(source, weight):
    return jnp.dot(source, weight, preferred_element_type=jnp.float32)


def backward_term(source, weight):
    return times_transpose(source, weight)


def gelu_value(values):
    return 0.5 * values * (1.0 + lax.erf(values * (1.0 / math.sqrt(2.0))))


def gelu_slope(values):
    return 0.5 * (1.0 + lax.erf(values * (1.0 / math.sqrt(2.0)))) + values * jnp.exp(
        -0.5 * values * values
    ) * (1.0 / math.sqrt(2.0 * math.pi))


def split_heads(matrix):
    return matrix.reshape(matrix.shape[0], -1, HEAD_DIM)


def head_scores(queries, key_rows, allowed):
    logits = jnp.einsum(
        "lhe,mhe->hlm",
        split_heads(queries),
        split_heads(key_rows),
        preferred_element_type=jnp.float32,
    ) * (1.0 / math.sqrt(HEAD_DIM))
    return jnp.where(allowed[None], logits, masked_score)


def attention_forward(queries, key_rows, values, allowed):
    scores = head_scores(queries, key_rows, allowed)
    highest = jnp.max(scores, axis=-1, keepdims=True)
    weights = jnp.exp(scores - highest)
    totals = jnp.sum(weights, axis=-1, keepdims=True)
    probability = (weights / totals).astype(jnp.bfloat16)
    context = jnp.einsum(
        "hlm,mhe->lhe", probability, split_heads(values), preferred_element_type=jnp.float32
    )
    return (
        context.reshape(queries.shape[0], -1).astype(jnp.bfloat16),
        (highest + jnp.log(totals))[..., 0],
    )


def attention_backward(queries, key_rows, values, allowed, log_total, upstream):
    scores = head_scores(queries, key_rows, allowed)
    probability = jnp.exp(scores - log_total[..., None])
    grad_heads = split_heads(upstream)
    grad_values = jnp.einsum(
        "hlm,lhe->mhe",
        probability.astype(jnp.bfloat16),
        grad_heads,
        preferred_element_type=jnp.float32,
    )
    grad_probs = jnp.einsum(
        "lhe,mhe->hlm", grad_heads, split_heads(values), preferred_element_type=jnp.float32
    )
    grad_scores = (
        probability * (grad_probs - jnp.sum(grad_probs * probability, axis=-1, keepdims=True))
    ).astype(jnp.bfloat16)
    score_scale = 1.0 / math.sqrt(HEAD_DIM)
    grad_queries = (
        jnp.einsum(
            "hlm,mhe->lhe", grad_scores, split_heads(key_rows), preferred_element_type=jnp.float32
        )
        * score_scale
    )
    grad_keys = (
        jnp.einsum(
            "hlm,lhe->mhe", grad_scores, split_heads(queries), preferred_element_type=jnp.float32
        )
        * score_scale
    )
    return (
        grad_queries.reshape(queries.shape[0], -1),
        grad_keys.reshape(key_rows.shape[0], -1),
        grad_values.reshape(key_rows.shape[0], -1),
    )


def shards(
    inputs,
    memory,
    prefix,
    self_qkv,
    self_bias,
    self_out,
    cross_qkv,
    cross_bias,
    cross_out,
    ffn_in,
    ffn_in_bias,
    ffn_out,
    norm_gain,
    norm_shift,
    out_bias,
    cotangent,
):
    groups = lax.axis_size("tensor")
    total_rows = inputs.shape[0]
    share_rows = total_rows // groups
    sequences = prefix.shape[0]
    seq_len = total_rows // sequences
    memory_len = memory.shape[0] // sequences
    offset_rows = lax.axis_index("tensor") * share_rows
    residual = lax.dynamic_slice_in_dim(inputs, offset_rows, share_rows, 0).astype(jnp.float32)
    gains = norm_gain.astype(jnp.float32)
    shifts = norm_shift.astype(jnp.float32)
    biases = out_bias.astype(jnp.float32)
    positions = jnp.arange(seq_len)
    causal = positions[None, :] <= positions[:, None]
    every_key = jnp.ones((seq_len, memory_len), dtype=bool)

    def by_sequence(matrix, length):
        return matrix.reshape(sequences, length, matrix.shape[-1])

    def self_allowed(limit):
        return causal | (positions[None, :] < limit)

    self_query = (
        jnp.dot(inputs, self_qkv[0], preferred_element_type=jnp.float32) + self_bias[0]
    ).astype(jnp.bfloat16)
    self_key = jnp.dot(inputs, self_qkv[1], preferred_element_type=jnp.float32).astype(jnp.bfloat16)
    self_value = (
        jnp.dot(inputs, self_qkv[2], preferred_element_type=jnp.float32) + self_bias[1]
    ).astype(jnp.bfloat16)
    self_pack = (
        by_sequence(self_query, seq_len),
        by_sequence(self_key, seq_len),
        by_sequence(self_value, seq_len),
    )

    def self_forward(packed):
        return attention_forward(packed[0], packed[1], packed[2], self_allowed(packed[3]))

    self_context, self_log = lax.map(self_forward, self_pack + (prefix,))
    self_context = self_context.reshape(total_rows, -1)
    self_branch = lax.psum_scatter(
        forward_term(self_context, self_out), "tensor", scatter_dimension=0, tiled=True
    )
    middle, middle_normed, middle_inverse = norm_forward(
        residual + self_branch + biases[:, 0], gains[:, 0], shifts[:, 0]
    )
    middle_rows = lax.all_gather(middle.astype(jnp.bfloat16), "tensor", axis=0, tiled=True)
    cross_query = (
        jnp.dot(middle_rows, cross_qkv[0], preferred_element_type=jnp.float32) + cross_bias[0]
    ).astype(jnp.bfloat16)
    cross_key = jnp.dot(memory, cross_qkv[1], preferred_element_type=jnp.float32).astype(
        jnp.bfloat16
    )
    cross_value = (
        jnp.dot(memory, cross_qkv[2], preferred_element_type=jnp.float32) + cross_bias[1]
    ).astype(jnp.bfloat16)
    cross_pack = (
        by_sequence(cross_query, seq_len),
        by_sequence(cross_key, memory_len),
        by_sequence(cross_value, memory_len),
    )

    def cross_forward(packed):
        return attention_forward(packed[0], packed[1], packed[2], every_key)

    cross_context, cross_log = lax.map(cross_forward, cross_pack)
    cross_context = cross_context.reshape(total_rows, -1)
    cross_branch = lax.psum_scatter(
        forward_term(cross_context, cross_out), "tensor", scatter_dimension=0, tiled=True
    )
    second, second_normed, second_inverse = norm_forward(
        middle + cross_branch + biases[:, 1], gains[:, 1], shifts[:, 1]
    )
    second_rows = lax.all_gather(second.astype(jnp.bfloat16), "tensor", axis=0, tiled=True)
    hidden_pre = jnp.dot(second_rows, ffn_in, preferred_element_type=jnp.float32) + ffn_in_bias
    hidden_act = gelu_value(hidden_pre).astype(jnp.bfloat16)
    ffn_branch = lax.psum_scatter(
        forward_term(hidden_act, ffn_out), "tensor", scatter_dimension=0, tiled=True
    )
    result, out_normed, out_inverse = norm_forward(
        second + ffn_branch + biases[:, 2], gains[:, 2], shifts[:, 2]
    )
    grad_third, gain_third, shift_third = norm_backward(
        cotangent.astype(jnp.float32), out_normed, out_inverse, gains[:, 2]
    )
    bias_third = jnp.sum(grad_third, axis=0)
    third_rows = lax.all_gather(grad_third.astype(jnp.bfloat16), "tensor", axis=0, tiled=True)
    ffn_out_grad = rows_product(hidden_act, third_rows)
    grad_pre = times_transpose(third_rows, ffn_out) * gelu_slope(hidden_pre)
    ffn_in_bias_grad = jnp.sum(grad_pre, axis=0)
    grad_pre_low = grad_pre.astype(jnp.bfloat16)
    ffn_in_grad = rows_product(second_rows, grad_pre_low)
    grad_second = grad_third + lax.psum_scatter(
        backward_term(grad_pre_low, ffn_in), "tensor", scatter_dimension=0, tiled=True
    )
    grad_mid_norm, gain_second, shift_second = norm_backward(
        grad_second, second_normed, second_inverse, gains[:, 1]
    )
    bias_second = jnp.sum(grad_mid_norm, axis=0)
    second_grad_rows = lax.all_gather(
        grad_mid_norm.astype(jnp.bfloat16), "tensor", axis=0, tiled=True
    )
    cross_out_grad = rows_product(cross_context, second_grad_rows)
    cross_upstream = times_transpose(second_grad_rows, cross_out).astype(jnp.bfloat16)

    def cross_backward(packed):
        return attention_backward(packed[0], packed[1], packed[2], every_key, packed[3], packed[4])

    cross_dq, cross_dk, cross_dv = lax.map(
        cross_backward, cross_pack + (cross_log, by_sequence(cross_upstream, seq_len))
    )
    cross_dq = cross_dq.reshape(total_rows, -1)
    cross_dk = cross_dk.reshape(memory.shape[0], -1)
    cross_dv = cross_dv.reshape(memory.shape[0], -1)
    cross_bias_grad = jnp.stack([jnp.sum(cross_dq, axis=0), jnp.sum(cross_dv, axis=0)])
    cross_dq_low = cross_dq.astype(jnp.bfloat16)
    cross_dk_low = cross_dk.astype(jnp.bfloat16)
    cross_dv_low = cross_dv.astype(jnp.bfloat16)
    cross_qkv_grad = jnp.stack(
        [
            rows_product(middle_rows, cross_dq_low),
            rows_product(memory, cross_dk_low),
            rows_product(memory, cross_dv_low),
        ]
    )
    middle_partial = times_transpose(cross_dq_low, cross_qkv[0])
    memory_partial = times_transpose(cross_dk_low, cross_qkv[1]) + times_transpose(
        cross_dv_low, cross_qkv[2]
    )
    middle_summed, memory_summed = (
        lax.psum_scatter(middle_partial, "tensor", scatter_dimension=0, tiled=True),
        lax.psum_scatter(memory_partial, "tensor", scatter_dimension=0, tiled=True),
    )
    memory_grad = memory_summed.astype(jnp.bfloat16)
    grad_middle = grad_mid_norm + middle_summed
    grad_first, gain_first, shift_first = norm_backward(
        grad_middle, middle_normed, middle_inverse, gains[:, 0]
    )
    bias_first = jnp.sum(grad_first, axis=0)
    first_grad_rows = lax.all_gather(grad_first.astype(jnp.bfloat16), "tensor", axis=0, tiled=True)
    self_out_grad = rows_product(self_context, first_grad_rows)
    self_upstream = times_transpose(first_grad_rows, self_out).astype(jnp.bfloat16)

    def self_backward(packed):
        return attention_backward(
            packed[0], packed[1], packed[2], self_allowed(packed[3]), packed[4], packed[5]
        )

    self_dq, self_dk, self_dv = lax.map(
        self_backward, self_pack + (prefix, self_log, by_sequence(self_upstream, seq_len))
    )
    self_dq = self_dq.reshape(total_rows, -1)
    self_dk = self_dk.reshape(total_rows, -1)
    self_dv = self_dv.reshape(total_rows, -1)
    self_bias_grad = jnp.stack([jnp.sum(self_dq, axis=0), jnp.sum(self_dv, axis=0)])
    self_dq_low = self_dq.astype(jnp.bfloat16)
    self_dk_low = self_dk.astype(jnp.bfloat16)
    self_dv_low = self_dv.astype(jnp.bfloat16)
    self_qkv_grad = jnp.stack(
        [
            rows_product(inputs, self_dq_low),
            rows_product(inputs, self_dk_low),
            rows_product(inputs, self_dv_low),
        ]
    )
    input_partial = (
        times_transpose(self_dq_low, self_qkv[0])
        + times_transpose(self_dk_low, self_qkv[1])
        + times_transpose(self_dv_low, self_qkv[2])
    )
    gain_stack = jnp.stack([gain_first, gain_second, gain_third], axis=1)
    shift_stack = jnp.stack([shift_first, shift_second, shift_third], axis=1)
    bias_stack = jnp.stack([bias_first, bias_second, bias_third], axis=1)
    input_summed = lax.psum_scatter(input_partial, "tensor", scatter_dimension=0, tiled=True)
    gain_part, shift_part, bias_part = (
        lax.psum_scatter(gain_stack, "tensor", scatter_dimension=0, tiled=True),
        lax.psum_scatter(shift_stack, "tensor", scatter_dimension=0, tiled=True),
        lax.psum_scatter(bias_stack, "tensor", scatter_dimension=0, tiled=True),
    )
    input_grad = (input_summed + grad_first).astype(jnp.bfloat16)
    summed = lax.psum(
        (
            self_qkv_grad,
            self_bias_grad,
            self_out_grad,
            cross_qkv_grad,
            cross_bias_grad,
            cross_out_grad,
            gain_part,
            shift_part,
            bias_part,
            ffn_in_grad,
            ffn_in_bias_grad,
            ffn_out_grad,
        ),
        "dp",
    )
    return (
        result.astype(jnp.bfloat16),
        input_grad,
        memory_grad,
        summed[0],
        summed[1],
        summed[2],
        summed[3],
        summed[4],
        summed[5],
        summed[9],
        summed[10],
        summed[11],
        summed[6],
        summed[7],
        summed[8],
    )


def solution(mesh):
    return jax.shard_map(
        shards,
        mesh=mesh,
        in_specs=(
            P("dp", None),
            P("dp", None),
            P("dp"),
            P(None, None, "tensor"),
            P(None, "tensor"),
            P("tensor", None),
            P(None, None, "tensor"),
            P(None, "tensor"),
            P("tensor", None),
            P(None, "tensor"),
            P("tensor"),
            P("tensor", None),
            P(),
            P(),
            P(),
            P(("dp", "tensor"), None),
        ),
        out_specs=(
            P(("dp", "tensor"), None),
            P(("dp", "tensor"), None),
            P(("dp", "tensor"), None),
            P(None, None, "tensor"),
            P(None, "tensor"),
            P("tensor", None),
            P(None, None, "tensor"),
            P(None, "tensor"),
            P("tensor", None),
            P(None, "tensor"),
            P("tensor"),
            P("tensor", None),
            P("tensor", None),
            P("tensor", None),
            P("tensor", None),
        ),
        check_vma=False,
    )
```

profile of v0, /device:TPU:0, one launch (start us, length us, event | category | flops | bytes accessed | tf_op | source)
XLA Modules:
  0.0 1203.6 jit_solution(5686442684510884766)
XLA Ops:
  16.3 7.4 fusion.90
  23.8 8.0 fusion
  31.8 7.4 fusion.35
  43.6 46.6 %reduce-scatter.17.cloned.1.call-done = f32[256,1024]{1,0:T(8,128)} async-done(((f32[1024,1024]{1,0:T(8,128)}), f32[256,1024]{1,0:T(8,128)}) %reduce-scatter.17.cloned.1.call-update) | async-done | bytes 1048592 | tf_op jit(solution)/shard_map/reduce_scatter | solution.py:184
  99.2 17.4 %all-gather.6.cloned.1.call-done = bf16[1024,1024]{1,0:T(8,128)(2,1)} async-done(((bf16[256,1024]{1,0:T(8,128)(2,1)}), bf16[1024,1024]{1,0:T(8,128)(2,1)}) %all-gather.6.cloned.1.call-update) | async-done | bytes 2097168 | tf_op jit(solution)/shard_map/all_gather | solution.py:190
  119.0 8.1 multiply_reduce_fusion.2
  127.2 8.5 fusion.1
  135.7 7.7 fusion.34
  147.0 44.6 %reduce-scatter.19.cloned.1.call-done = f32[256,1024]{1,0:T(8,128)} async-done(((f32[1024,1024]{1,0:T(8,128)}), f32[256,1024]{1,0:T(8,128)}) %reduce-scatter.19.cloned.1.call-update) | async-done | bytes 1048592 | tf_op jit(solution)/shard_map/reduce_scatter | solution.py:211
  195.4 22.2 %all-gather.8.cloned.1.call-done = bf16[1024,1024]{1,0:T(8,128)(2,1)} async-done(((bf16[256,1024]{1,0:T(8,128)(2,1)}), bf16[1024,1024]{1,0:T(8,128)(2,1)}) %all-gather.8.cloned.1.call-update) | async-done | bytes 2097168 | tf_op jit(solution)/shard_map/all_gather | solution.py:217
  217.7 5.9 multiply_convert_fusion.2
  229.3 44.6 %reduce-scatter.21.cloned.1.call-done = f32[256,1024]{1,0:T(8,128)} async-done(((f32[1024,1024]{1,0:T(8,128)}), f32[256,1024]{1,0:T(8,128)}) %reduce-scatter.21.cloned.1.call-update) | async-done | bytes 1048592 | tf_op jit(solution)/shard_map/reduce_scatter | solution.py:220
  280.2 22.7 %all-gather.10.cloned.1.call-done = bf16[1024,1024]{1,0:T(8,128)(2,1)} async-done(((bf16[256,1024]{1,0:T(8,128)(2,1)}), bf16[1024,1024]{1,0:T(8,128)(2,1)}) %all-gather.10.cloned.1.call-update) | async-done | bytes 2097168 | tf_op jit(solution)/shard_map/all_gather | solution.py:230
  302.9 7.1 fusion.91
  311.3 4.4 fusion.42
  315.8 44.6 %reduce-scatter.23.cloned.1.call-done = f32[256,1024]{1,0:T(8,128)} async-done(((f32[1024,1024]{1,0:T(8,128)}), f32[256,1024]{1,0:T(8,128)}) %reduce-scatter.23.cloned.1.call-update) | async-done | bytes 1048592 | tf_op jit(solution)/shard_map/reduce_scatter | solution.py:236
  364.9 22.5 %all-gather.12.cloned.1.call-done = bf16[1024,1024]{1,0:T(8,128)(2,1)} async-done(((bf16[256,1024]{1,0:T(8,128)(2,1)}), bf16[1024,1024]{1,0:T(8,128)(2,1)}) %all-gather.12.cloned.1.call-update) | async-done | bytes 2097168 | tf_op jit(solution)/shard_map/all_gather | solution.py:243
  389.9 15.5 %multiply_reduce_fusion.1 = (f32[4,1024]{1,0:T(4,128)S(1)}, f32[4,1024,1024]{1,2,0:T(8,128)}) fusion(f32[4,1024,1024]{1,2,0:T(8,128)} %get-tuple-element.216, f32[4,1024]{1,0:T(4,128)S(1)} %log_add_fusion, bf16[1024,4,64]{0,2,1:T(8,128)(2,1)S(1)} %bitcast.205, bf16[1024,4,64]{0,2,1:T(8,128)(2,1)S(1)} %bitcast.214), kind=kOutput, calls=%fused_computation.3 | convolution fusion | flops 553644032 | bytes 34635776 | tf_op jit(solution)/shard_map/while/body/eval_jaxpr/lhe,mhe->hlm/dot_general | solution.py:101
  406.4 8.0 multiply_convert_fusion.1
  422.5 44.6 %reduce-scatter.25.cloned.1.call-done = f32[256,1024]{1,0:T(8,128)} async-done(((f32[1024,1024]{1,0:T(8,128)}), f32[256,1024]{1,0:T(8,128)}) %reduce-scatter.25.cloned.1.call-update) | async-done | bytes 1048592 | tf_op jit(solution)/shard_map/reduce_scatter | solution.py:274
  470.3 6.2 fusion.33
  477.6 8.4 fusion.84
  495.6 8.7 fusion.86
  504.3 13.9 %multiply_reduce_fusion = (f32[4,1024]{1,0:T(4,128)S(1)}, f32[4,1024,1024]{1,2,0:T(8,128)}) fusion(f32[4,1024,1024]{1,2,0:T(8,128)} %get-tuple-element.214, f32[4,1024]{1,0:T(4,128)S(1)} %log_add_fusion.1, bf16[1024,4,64]{0,2,1:T(8,128)(2,1)S(1)} %bitcast.208, bf16[1024,4,64]{0,2,1:T(8,128)(2,1)S(1)} %bitcast.212), kind=kOutput, calls=%fused_computation.1 | convolution fusion | flops 549449728 | bytes 34635776 | tf_op jit(solution)/shard_map/while/body/eval_jaxpr/lhe,mhe->hlm/dot_general | solution.py:101
  519.0 8.0 multiply_convert_fusion
  537.3 6.1 fusion.97
  543.4 4.5 fusion.40
  565.8 23.3 %reduce-scatter.31.cloned.1.call-done = f32[256,3]{1,0:T(8,128)} async-done(((f32[1024,3]{1,0:T(8,128)}), f32[256,3]{1,0:T(8,128)}) %reduce-scatter.31.cloned.1.call-update) | async-done | bytes 3088
  590.1 23.1 %reduce-scatter.35.cloned.1.call-done = f32[256,3]{1,0:T(8,128)} async-done(((f32[1024,3]{1,0:T(8,128)}), f32[256,3]{1,0:T(8,128)}) %reduce-scatter.35.cloned.1.call-update) | async-done | bytes 3088
  614.4 37.7 %all-reduce = (f32[2,256]{1,0:T(2,128)}, f32[2,256]{1,0:T(2,128)}, f32[1024]{0:T(1024)}, f32[256,3]{0,1:T(4,128)}, f32[256,3]{0,1:T(4,128)}, /*index=5*/f32[256,3]{0,1:T(4,128)}) all-reduce(f32[2,256]{1,0:T(2,128)S(1)} %pad_maximum_fusion.5, f32[2,256]{1,0:T(2,128)S(1)} %pad_maximum_fusion.6, ...), channel_id=1, replica_groups=mesh['dp'=8,'tensor'=4] {'dp'}, use_global_device_ids=true, to_apply=%region_28.29 | all-reduce | flops 4352 | bytes 34816 | tf_op jit(solution)/shard_map/psum | solution.py:324
  652.0 8.8 reduce-scatter.27.cloned.1.call-done
  663.0 518.4 %all-reduce.4.cloned.1.call-done = (f32[3,1024,256]{1,2,0:T(8,128)}, f32[256,1024]{1,0:T(8,128)}, f32[3,1024,256]{2,1,0:T(8,128)}, f32[256,1024]{1,0:T(8,128)}, ...) async-done(((f32[3,1024,256]{1,2,0:T(8,128)}, f32[256,1024]{1,0:T(8,128)}, f32[3,1024,256]{2,1,0:T(8,128)}, f32[256,1024]{1,0:T(8,128)}, f32[1024,1024]{1,0:T(8,128)}, ...) | async-done | bytes 16777232 | tf_op jit(solution)/shard_map/psum | solution.py:324
  (286 shorter events, 122.4 us)
Async XLA Ops:
  7.2 210.5 %copy-start = (bf16[1024,1024]{1,0:T(8,128)(2,1)S(1)}, bf16[1024,1024]{1,0:T(8,128)(2,1)}, u32[]{:S(2)}) copy-start(bf16[1024,1024]{1,0:T(8,128)(2,1)} %param.25) | copy-start | bytes 6291460
  7.2 83.0 %reduce-scatter.17.cloned.1.call-start = ((), (), s32[]{:S(2)}) async-start(), calls=%async_computation.10 | async-start | bytes 5242880 | tf_op jit(solution)/shard_map/reduce_scatter | solution.py:184
  13.9 17.8 %copy-start.43 = (bf16[1024,256]{0,1:T(8,128)(2,1)}, bf16[1024,256]{0,1:T(8,128)(2,1)S(1)}, u32[]{:S(2)}) copy-start(bf16[1024,256]{0,1:T(8,128)(2,1)S(1)} %fusion.28) | copy-start | bytes 1572868
  42.8 51.3 %copy-start.62 = (bf16[2,256]{1,0:T(2,128)(2,1)S(1)}, bf16[2,256]{1,0:T(2,128)(2,1)}, u32[]{:S(2)}) copy-start(bf16[2,256]{1,0:T(2,128)(2,1)} %param.23) | copy-start | bytes 3076
  42.9 73.7 %all-gather.6.cloned.1.call-start = ((), (), s32[]{:S(2)}) async-start(), calls=%async_computation.11 | async-start | bytes 2621440 | tf_op jit(solution)/shard_map/all_gather | solution.py:190
  93.9 97.8 %reduce-scatter.19.cloned.1.call-start = ((), (), s32[]{:S(2)}) async-start(), calls=%async_computation.12 | async-start | bytes 5242880 | tf_op jit(solution)/shard_map/reduce_scatter | solution.py:211
  96.6 30.6 %copy-start.26 = (bf16[1024,256]{0,1:T(8,128)(2,1)}, bf16[1024,256]{0,1:T(8,128)(2,1)S(1)}, u32[]{:S(2)}) copy-start(bf16[1024,256]{0,1:T(8,128)(2,1)S(1)} %convolution_convert_fusion.2) | copy-start | bytes 1572868
  99.2 36.5 %copy-start.45 = (bf16[1024,256]{0,1:T(8,128)(2,1)}, bf16[1024,256]{0,1:T(8,128)(2,1)S(1)}, u32[]{:S(2)}) copy-start(bf16[1024,256]{0,1:T(8,128)(2,1)S(1)} %fusion.30) | copy-start | bytes 1572868
  147.0 48.4 %copy-start.63 = (bf16[1024]{0:T(1024)(128)(2,1)S(1)}, bf16[1024]{0:T(1024)(128)(2,1)}, u32[]{:S(2)}) copy-start(bf16[1024]{0:T(1024)(128)(2,1)} %param.26) | copy-start | bytes 6148
  147.0 70.7 %all-gather.8.cloned.1.call-start = ((), (), s32[]{:S(2)}) async-start(), calls=%async_computation.13 | async-start | bytes 2621440 | tf_op jit(solution)/shard_map/all_gather | solution.py:217
  195.0 79.0 %reduce-scatter.21.cloned.1.call-start = ((), (), s32[]{:S(2)}) async-start(), calls=%async_computation.14 | async-start | bytes 5242880 | tf_op jit(solution)/shard_map/reduce_scatter | solution.py:220
  229.3 73.6 %all-gather.10.cloned.1.call-start = ((), (), s32[]{:S(2)}) async-start(), calls=%async_computation.15 | async-start | bytes 2621440 | tf_op jit(solution)/shard_map/all_gather | solution.py:230
  280.1 80.3 %reduce-scatter.23.cloned.1.call-start = ((), (), s32[]{:S(2)}) async-start(), calls=%async_computation.16 | async-start | bytes 5242880 | tf_op jit(solution)/shard_map/reduce_scatter | solution.py:236
  315.7 44.7 %copy-start.10 = (f32[256,1024]{1,0:T(8,128)S(1)}, f32[256,1024]{1,0:T(8,128)}, u32[]{:S(2)}) copy-start(f32[256,1024]{1,0:T(8,128)} %copy-done.9) | copy-start | bytes 3145732
  315.8 71.6 %all-gather.12.cloned.1.call-start = ((), (), s32[]{:S(2)}) async-start(), calls=%async_computation.17 | async-start | bytes 2621440 | tf_op jit(solution)/shard_map/all_gather | solution.py:243
  363.7 26.1 %copy-start.46 = (bf16[1024,256]{0,1:T(8,128)(2,1)S(1)}, bf16[1024,256]{0,1:T(8,128)(2,1)}, u32[]{:S(2)}) copy-start(bf16[1024,256]{0,1:T(8,128)(2,1)} %copy-done.45) | copy-start | bytes 1572868
  364.6 102.5 %reduce-scatter.25.cloned.1.call-start = ((), (), s32[]{:S(2)}) async-start(), calls=%async_computation.18 | async-start | bytes 5242880 | tf_op jit(solution)/shard_map/reduce_scatter | solution.py:274
  389.9 16.6 %slice-start.7 = ((s8[16777216]{0:T(1024)(128)(4,1)}), s8[4194304]{0:T(1024)(128)(4,1)S(1)}, s32[]{:S(2)}) async-start(s8[16777216]{0:T(1024)(128)(4,1)} %bitcast.181), calls=%async_computation.33 | async-start | bytes 8388608
  418.5 48.6 %copy-start.4 = (f32[256,1024]{1,0:T(8,128)S(1)}, f32[256,1024]{1,0:T(8,128)}, u32[]{:S(2)}) copy-start(f32[256,1024]{1,0:T(8,128)} %copy-done.3) | copy-start | bytes 3145732
  422.4 47.9 %copy-start.25 = (bf16[1024,256]{0,1:T(8,128)(2,1)S(1)}, bf16[1024,256]{0,1:T(8,128)(2,1)}, u32[]{:S(2)}) copy-start(bf16[1024,256]{0,1:T(8,128)(2,1)} %copy-done.24) | copy-start | bytes 1572868
  422.4 70.8 %all-gather.14.cloned.1.call-start = ((), (), s32[]{:S(2)}) async-start(), calls=%async_computation.19 | async-start | bytes 2621440 | tf_op jit(solution)/shard_map/all_gather | solution.py:283
  470.2 91.6 %reduce-scatter.29.cloned.1.call-start = ((), (), s32[]{:S(2)}) async-start(), calls=%async_computation.21 | async-start | bytes 5242880 | tf_op jit(solution)/shard_map/reduce_scatter | solution.py:275
  488.9 76.0 %reduce-scatter.33.cloned.1.call-start = ((), (), s32[]{:S(2)}) async-start(), calls=%async_computation.23 | async-start | bytes 655360
  490.6 98.5 %reduce-scatter.31.cloned.1.call-start = ((), (), s32[]{:S(2)}) async-start(), calls=%async_computation.22 | async-start | bytes 655360
  491.8 121.4 %reduce-scatter.35.cloned.1.call-start = ((), (), s32[]{:S(2)}) async-start(), calls=%async_computation.24 | async-start | bytes 655360
  492.9 167.9 %reduce-scatter.27.cloned.1.call-start = ((), (), s32[]{:S(2)}) async-start(), calls=%async_computation.20 | async-start | bytes 5242880 | tf_op jit(solution)/shard_map/reduce_scatter | solution.py:317
  495.6 22.7 %slice-start = ((s8[16777216]{0:T(1024)(128)(4,1)}), s8[4194304]{0:T(1024)(128)(4,1)S(1)}, s32[]{:S(2)}) async-start(s8[16777216]{0:T(1024)(128)(4,1)} %bitcast.179), calls=%async_computation.26 | async-start | bytes 8388608
  495.6 22.7 %slice-start.1 = ((s8[16777216]{0:T(1024)(128)(4,1)}), s8[4194304]{0:T(1024)(128)(4,1)S(1)}, s32[]{:S(2)}) async-start(s8[16777216]{0:T(1024)(128)(4,1)} %bitcast.179), calls=%async_computation.27 | async-start | bytes 8388608
  504.3 28.6 %copy-start.16 = (bf16[1024,4,64]{0,2,1:T(8,128)(2,1)}, bf16[1024,4,64]{0,2,1:T(8,128)(2,1)S(1)}, u32[]{:S(2)}) copy-start(bf16[1024,4,64]{0,2,1:T(8,128)(2,1)S(1)} %get-tuple-element.199) | copy-start | bytes 1572868
  535.7 645.7 %all-reduce.4.cloned.1.call-start = ((), (), s32[]{:S(2)}) async-start(), calls=%async_computation.25 | async-start | bytes 33554432 | tf_op jit(solution)/shard_map/psum | solution.py:324
  561.0 53.4 %copy-start.61 = (f32[1024]{0:T(1024)S(1)}, f32[1024]{0:T(1024)}, u32[]{:S(2)}) copy-start(f32[1024]{0:T(1024)} %get-tuple-element.227) | copy-start | bytes 12292
  561.0 99.9 %copy-start.8 = (f32[256,1024]{1,0:T(8,128)S(1)}, f32[256,1024]{1,0:T(8,128)}, u32[]{:S(2)}) copy-start(f32[256,1024]{1,0:T(8,128)} %copy-done.7) | copy-start | bytes 3145732
  (63 other events, 296.2 us)
Sparse Core Ops, SparseCore 0:
  43.0 47.2 reduce-scatter.16
  94.0 22.5 all-gather.5
  147.1 44.5 reduce-scatter.18
  195.1 22.5 all-gather.7
  229.4 44.4 reduce-scatter.20
  280.3 22.5 all-gather.9
  315.9 44.4 reduce-scatter.22
  364.8 22.5 all-gather.11
  422.6 44.4 reduce-scatter.24
  470.4 22.5 all-gather.13
  496.3 44.4 reduce-scatter.28
  543.1 21.6 reduce-scatter.32
  567.5 21.6 reduce-scatter.30
  591.5 21.6 reduce-scatter.34
  616.3 44.4 reduce-scatter.26
  666.8 514.5 all-reduce.3
where the time goes:
time: 1210 us; the launch traced here: 1200 us
  waiting for transfers between devices  885 us (73%)
  matrix products  168 us (14%)
  other arithmetic  60.3 us (5%)
  blocking collectives  37.7 us (3%)
  local copies, waits for them, and re-layouts  35.2 us (3%)
  between operations  16.2 us (1%)
    psum x1, waiting for transfers between devices, shards(): lax.psum((self_qkv_grad, self_bias_grad, self_out_grad, cross_qkv_grad, c...  518 us
    unnamed x19, waiting for transfers between devices  47.6 us
    reduce_scatter x1, waiting for transfers between devices, shards(): lax.psum_scatter(forward_term(self_context, self_out), 'tensor', scatter_...  46.6 us
    reduce_scatter x1, waiting for transfers between devices, shards(): lax.psum_scatter(forward_term(cross_context, cross_out), 'tensor', scatte...  44.6 us
    reduce_scatter x1, waiting for transfers between devices, shards(): lax.psum_scatter(forward_term(hidden_act, ffn_out), 'tensor', scatter_dim...  44.6 us
    reduce_scatter x1, waiting for transfers between devices, shards(): lax.psum_scatter(middle_partial, 'tensor', scatter_dimension=0, tiled=True)  44.6 us
    reduce_scatter x1, waiting for transfers between devices, shards(): lax.psum_scatter(backward_term(grad_pre_low, ffn_in), 'tensor', scatter_d...  44.6 us
    psum x1, blocking collectives, shards(): lax.psum((self_qkv_grad, self_bias_grad, self_out_grad, cross_qkv_grad, c...  37.7 us
  transfers between devices with their start and end apart: 16, of which 14 were waited for; matrix products, arithmetic and copies ran while one was open for 8% of the time, Pallas kernels for 0%

commit v1 on v0

v1 whole, which is shorter than its diff:
```python
import functools
import math

import jax
import jax.numpy as jnp
from jax import lax
from jax.experimental import pallas as pl
from jax.experimental.pallas import tpu as pltpu
from jax.sharding import PartitionSpec as P

HEAD_DIM = 64
EPS = 1e-05
MASKED = -1e30
F32 = jnp.float32
BF16 = jnp.bfloat16
MESH = pl.DeviceIdType.MESH
ANY = pl.BlockSpec(memory_space=pl.ANY)
VMEM = pl.BlockSpec(memory_space=pltpu.VMEM)
SMEM = pl.BlockSpec(memory_space=pltpu.SMEM)
NN = (((1,), (0,)), ((), ()))
NT = (((1,), (1,)), ((), ()))
TN = (((0,), (0,)), ((), ()))


def mm(a, b, dims=NN):
    return lax.dot_general(a, b, dims, preferred_element_type=F32)


def fold(v):
    return jnp.sum(v.reshape(-1, 8, v.shape[-1]), axis=0)


def layer_kernel(
    T, D, HC, FF,
    x_hbm, mem_hbm, prefix_ref, wsq_hbm, wso_hbm, wcq_hbm, wco_hbm, w1_hbm, w2_hbm, cot_hbm,
    norm_ref, sbias_ref, cbias_ref, fbias_ref,
    out_hbm, ig_hbm, mg_hbm, gsq_hbm, gso_hbm, gcq_hbm, gco_hbm, g1_hbm, g2_hbm, small_ref,
    xin, mem, wsq, wso, wcq, wco, w1, w2, cot,
    q1, k1, v1, c1, q2, k2, v2, c2, lse1, lse2,
    mlow, slow, d3l, d2l, act, slope, dpre,
    n1, n2, inv1, inv2, dcur,
    chip_send, chip_recv, acc, x_send, x_recv,
    dql, dkl, dvl, kT, dqT, qm, dom, up, G,
    sums, fsum, hsum,
    in_sems, out_sems, cs_sem, cr_sem, xs_sem, xr_sem, as_sem, ar_sem,
):
    H = HC // HEAD_DIM
    obuf = cot
    units = [(G, u * (T // 4)) for u in range(8)] + [(slow, u * (T // 4)) for u in range(4)] + [
        (w1, u * (T // 4)) for u in range(4)]
    CH = T // 2
    R = T // 4
    dp = lax.axis_index("dp")
    tn = lax.axis_index("tensor")
    xi = tn // 2
    ci = lax.rem(tn, 2)
    mate = (dp, xi * 2 + (1 - ci))
    peer = (dp, (1 - xi) * 2 + ci)

    srcs = [(x_hbm, xin), (wsq_hbm, wsq), (wso_hbm, wso), (mem_hbm, mem), (wcq_hbm, wcq), (wco_hbm, wco),
            (w1_hbm, w1), (w2_hbm, w2)]
    loads = [pltpu.make_async_copy(a, b, in_sems.at[i]) for i, (a, b) in enumerate(srcs)]
    loads.append(pltpu.make_async_copy(cot_hbm, cot.at[xi], in_sems.at[len(srcs)]))
    for load in loads:
        load.start()
    XIN, WSQ, WSO, MEMR, WCQ, WCO, W1, W2, COT = range(9)

    barrier = pltpu.get_barrier_semaphore()
    for other in (mate, peer):
        pl.semaphore_signal(barrier, inc=1, device_id=other, device_id_type=MESH)
    pl.semaphore_wait(barrier, 2)

    loads[COT].wait()
    cot_copy = pltpu.make_async_remote_copy(
        src_ref=cot.at[xi], dst_ref=cot.at[xi], send_sem=xs_sem.at[0, 0], recv_sem=xr_sem.at[0, 0],
        device_id=peer, device_id_type=MESH)
    cot_copy.start()

    sums[...] = jnp.zeros_like(sums)
    fsum[...] = jnp.zeros_like(fsum)
    hsum[...] = jnp.zeros_like(hsum)

    def mine(j):
        return pl.multiple_of(j * CH + ci * R, R)

    def mates(j):
        return pl.multiple_of(j * CH + (1 - ci) * R, R)

    def head_mask(h):
        lane = lax.broadcasted_iota(jnp.int32, (8, HC), 1)
        return jnp.where(lane // HEAD_DIM == h, 1.0, 0.0)[0:1].astype(BF16)

    def project(src, w, wi, bias, dst, r0, n, scale=None):
        @pl.loop(0, n // R)
        def _(i):
            r = pl.multiple_of(r0 + i * R, R)
            y = mm(src[pl.ds(r, R), :], w[wi])
            if bias is not None:
                y = y + bias
            y = y.astype(BF16)
            if scale is not None:
                y = y * jnp.asarray(scale, BF16)
            dst[pl.ds(r, R), :] = y

    SC = 1.0 / math.sqrt(HEAD_DIM)

    def visible(keys_first, r0, nk):
        if keys_first:
            shape, kd = (nk, R), 0
        else:
            shape, kd = (R, nk), 1
        key = lax.broadcasted_iota(jnp.int32, shape, kd)
        row = lax.broadcasted_iota(jnp.int32, shape, 1 - kd) + r0
        return (key <= row) | (key < prefix_ref[0])

    def attend(q, k, v, c, lse, j, causal):
        for i in range(CH // R):
            r0 = j * CH + i * R
            nk = max(T // 2, r0 + R) if causal else T
            rows = slice(r0, r0 + R)
            lane = lax.broadcasted_iota(jnp.int32, (R, 128), 1)
            for h in range(H):
                m = head_mask(h)
                s = mm(q[rows, :] * m, k[:nk, :], NT)
                if causal:
                    s = jnp.where(visible(False, r0, nk), s, MASKED)
                top = jnp.max(s, axis=1, keepdims=True)
                e = jnp.exp(s - top)
                tot = jnp.sum(e, axis=1, keepdims=True)
                p = (e * (1.0 / tot)).astype(BF16)
                o = mm(p, v[:nk, :] * m)
                l = top + jnp.log(tot)
                if h == 0:
                    dqT[...] = o
                    stat = jnp.where(lane == h, l, 0.0)
                else:
                    dqT[...] += o
                    stat = jnp.where(lane == h, l, stat)
            c[rows, :] = dqT[...].astype(BF16)
            lse[:, rows] = jnp.transpose(stat)[0:8, :]

    def attend_back(q, k, v, lse, j, causal, dk, dv, first, slot):
        pbuf, sbuf = act, dpre
        for i in range(CH // R):
            r0 = j * CH + i * R
            nk = max(T // 2, r0 + R) if causal else T
            rows = slice(r0, r0 + R)

            @pl.loop(0, H)
            def _(h):
                m = head_mask(h)
                qh = q[rows, :] * m
                doh = up[i * R:(i + 1) * R, :] * m
                cols = pl.ds(pl.multiple_of(h * R, R), R)
                qm[cols, :] = qh
                dom[cols, :] = doh
                s = mm(k[:nk, :], qh, NT)
                if causal:
                    s = jnp.where(visible(True, r0, nk), s, MASKED)
                p = jnp.exp(s - lse[pl.ds(h, 1), rows])
                dpv = mm(v[:nk, :], doh, NT)
                dd = jnp.sum(p * dpv, axis=0, keepdims=True)
                ds = (p * (dpv - dd)).astype(BF16)
                pbuf[:nk, cols] = p.astype(BF16)
                sbuf[:nk, cols] = ds
                hr = pl.ds(pl.multiple_of(h * HEAD_DIM, HEAD_DIM), HEAD_DIM)
                dqT[hr, :] = mm(kT[hr, :nk], ds)

            @pl.loop(0, nk // R)
            def _(kt):
                kr = pl.ds(pl.multiple_of(kt * R, R), R)
                a = mm(pbuf[kr, :], dom[...])
                b = mm(sbuf[kr, :], qm[...])
                if first and i == 0:
                    dv[kr, :] = a
                    dk[kr, :] = b
                else:
                    dv[kr, :] += a
                    dk[kr, :] += b

            if first and i == 0 and nk < T:
                dv[nk:, :] = jnp.zeros((T - nk, HC), F32)
                dk[nk:, :] = jnp.zeros((T - nk, HC), F32)
            dq = jnp.transpose(dqT[...]) * SC
            hsum[slot] += fold(dq)
            dql[rows, :] = dq.astype(BF16)

    def finish_back(dk, dv, slot):
        @pl.loop(0, T // R)
        def _(i):
            r = pl.ds(pl.multiple_of(i * R, R), R)
            a = dv[r, :]
            hsum[slot + 1] += fold(a)
            dvl[r, :] = a.astype(BF16)
            dkl[r, :] = dk[r, :].astype(BF16)

    def chip_copy(s, j):
        dst = mlow.at[pl.ds(j * R, R)] if s == 7 else chip_recv.at[j]
        return pltpu.make_async_remote_copy(
            src_ref=chip_send.at[j], dst_ref=dst, send_sem=cs_sem.at[s, j], recv_sem=cr_sem.at[s, j],
            device_id=mate, device_id_type=MESH)

    def x_copy(s, j):
        return pltpu.make_async_remote_copy(
            src_ref=x_send.at[j], dst_ref=x_recv.at[s % 2, j], send_sem=xs_sem.at[s, j], recv_sem=xr_sem.at[s, j],
            device_id=peer, device_id_type=MESH)

    def low_copy(s, j, low):
        rows = pl.ds(mine(j), R)
        return pltpu.make_async_remote_copy(
            src_ref=low.at[rows], dst_ref=low.at[rows], send_sem=as_sem.at[s, j], recv_sem=ar_sem.at[s, j],
            device_id=mate, device_id_type=MESH)

    NTILE = 256

    def partial(s, j, terms):
        def tile(r, n):
            y = None
            for lhs, rhs, dims in terms:
                t = mm(lhs[pl.ds(r, R), :], rhs(n), dims)
                y = t if y is None else y + t
            return y

        @pl.loop(0, D // NTILE)
        def _(n):
            n = pl.ds(pl.multiple_of(n * NTILE, NTILE), NTILE)
            chip_send[j, :, n] = tile(mates(j), n).astype(BF16)

        chip_copy(s, j).start()

        @pl.loop(0, D // NTILE)
        def _(n):
            n = pl.ds(pl.multiple_of(n * NTILE, NTILE), NTILE)
            acc[j, :, n] = tile(mine(j), n)

    RT = 32

    def chip_sum(s, j):
        chip_copy(s, j).wait()

        @pl.loop(0, R // RT)
        def _(i):
            r = pl.ds(pl.multiple_of(i * RT, RT), RT)
            x_send[j, r, :] = (acc[j, r, :] + chip_recv[j, r, :].astype(F32)).astype(BF16)

        x_copy(s, j).start()

    def total(s, j, r):
        return x_send[j, r, :].astype(F32) + x_recv[s % 2, j, r, :].astype(F32)

    def gain(i):
        return norm_ref[i:i + 1, :]

    def shift(i):
        return norm_ref[3 + i:4 + i, :]

    def obias(i):
        return norm_ref[6 + i:7 + i, :]

    def normed(v):
        cen = v - jnp.mean(v, axis=-1, keepdims=True)
        inv = lax.rsqrt(jnp.mean(cen * cen, axis=-1, keepdims=True) + EPS)
        return cen * inv, inv

    def norm_back(dy, n, inv, i):
        g = dy * gain(i)
        dv = inv * (g - jnp.mean(g, axis=-1, keepdims=True) - n * jnp.mean(g * n, axis=-1, keepdims=True))
        sums[i] += fold(dy * n)
        sums[3 + i] += fold(dy)
        sums[6 + i] += fold(dv)
        return dv

    def finish(s, j, low):
        x_copy(s, j).wait()
        base = mine(j)

        @pl.loop(0, R // RT)
        def _(i):
            r = pl.ds(pl.multiple_of(i * RT, RT), RT)
            g = pl.ds(pl.multiple_of(base + i * RT, RT), RT)
            t = total(s, j, r)
            if s == 1:
                n, inv = normed(xin[g, :].astype(F32) + t + obias(0))
                n1[j, r, :] = n
                inv1[j, r, :] = jnp.broadcast_to(inv, (RT, 128))
                low[g, :] = (n * gain(0) + shift(0)).astype(BF16)
            elif s == 2:
                n, inv = normed(n1[j, r, :] * gain(0) + shift(0) + t + obias(1))
                n2[j, r, :] = n
                inv2[j, r, :] = jnp.broadcast_to(inv, (RT, 128))
                low[g, :] = (n * gain(1) + shift(1)).astype(BF16)
            elif s == 3:
                n, inv = normed(n2[j, r, :] * gain(1) + shift(1) + t + obias(2))
                dy = cot[j, r, :].astype(F32)
                obuf[j, r, :] = (n * gain(2) + shift(2)).astype(BF16)
                d = norm_back(dy, n, inv, 2)
                dcur[j, r, :] = d
                low[g, :] = d.astype(BF16)
            elif s == 4:
                d = norm_back(dcur[j, r, :] + t, n2[j, r, :], inv2[j, r, 0:1], 1)
                dcur[j, r, :] = d
                low[g, :] = d.astype(BF16)
            else:
                d = norm_back(dcur[j, r, :] + t, n1[j, r, :], inv1[j, r, 0:1], 0)
                dcur[j, r, :] = d
                low[g, :] = d.astype(BF16)

        low_copy(s, j, low).start()

    def gather(s, j, low):
        low_copy(s, j, low).wait()

    def got(s, j, i):
        if s == 7:
            return mlow[pl.ds(pl.multiple_of(j * R + i * RT, RT), RT), :].astype(F32)
        return chip_recv[j, pl.ds(pl.multiple_of(i * RT, RT), RT), :].astype(F32)

    def scatter_send(s):
        for j in range(2):
            chip_copy(s, j).wait()
        j = 1 - xi

        @pl.loop(0, R // RT)
        def _(i):
            r = pl.ds(pl.multiple_of(i * RT, RT), RT)
            x_send[0, r, :] = (acc[j, r, :] + got(s, j, i)).astype(BF16)

        x_copy(s, 0).start()

    def scatter_finish(s, extra, dst):
        x_copy(s, 0).wait()

        @pl.loop(0, R // RT)
        def _(i):
            r = pl.ds(pl.multiple_of(i * RT, RT), RT)
            t = acc[xi, r, :] + got(s, xi, i) + x_recv[s % 2, 0, r, :].astype(F32)
            if extra is not None:
                t = t + extra[xi, r, :]
            dst[r, :] = t.astype(BF16)

    def grad_rows(u, lhs, c0, rhs):
        @pl.loop(0, D // NTILE)
        def _(n):
            n = pl.ds(pl.multiple_of(n * NTILE, NTILE), NTILE)
            unit, r0 = units[u]
            unit[r0:r0 + R, n] = mm(lhs[:, pl.ds(c0, R)], rhs[:, n], TN).astype(BF16)

    def grad_cols(pairs, lhs):
        @pl.loop(0, D // R)
        def _(b):
            cols = pl.ds(pl.multiple_of(b * R, R), R)
            for u, rhs in pairs:
                unit, r0 = units[u]
                unit[r0:r0 + R, cols] = mm(lhs[:, cols], rhs[...], TN).astype(BF16)

    loads[XIN].wait()
    loads[WSQ].wait()
    project(xin, wsq, 0, sbias_ref[0:1, :], q1, 0, T, SC)
    project(xin, wsq, 1, None, k1, 0, T)
    project(xin, wsq, 2, sbias_ref[1:2, :], v1, 0, T)
    loads[WSO].wait()

    def self_forward(j):
        attend(q1, k1, v1, c1, lse1, j, True)
        partial(1, j, [(c1, lambda n: wso[:, n], NN)])
        chip_sum(1, j)

    def cross_forward(j):
        project(mlow, wcq, 0, cbias_ref[0:1, :], q2, j * CH, CH, SC)
        attend(q2, k2, v2, c2, lse2, j, False)
        partial(2, j, [(c2, lambda n: wco[:, n], NN)])
        chip_sum(2, j)

    def ffn_forward(j):
        @pl.loop(0, CH // R)
        def _(i):
            r = pl.ds(pl.multiple_of(j * CH + i * R, R), R)

            @pl.loop(0, FF // NTILE)
            def _(n):
                cols = pl.ds(pl.multiple_of(n * NTILE, NTILE), NTILE)
                pre = mm(slow[r, :], w1[:, cols]) + fbias_ref[:, cols]
                half = 0.5 * (1.0 + lax.erf(pre * (1.0 / math.sqrt(2.0))))
                act[r, cols] = (pre * half).astype(BF16)
                slope[n, r, :] = half + pre * jnp.exp(-0.5 * pre * pre) * (1.0 / math.sqrt(2.0 * math.pi))

        partial(3, j, [(act, lambda n: w2[:, n], NN)])
        chip_sum(3, j)

    def ffn_backward(j):
        @pl.loop(0, CH // R)
        def _(i):
            r = pl.ds(pl.multiple_of(j * CH + i * R, R), R)

            @pl.loop(0, FF // NTILE)
            def _(n):
                cols = pl.ds(pl.multiple_of(n * NTILE, NTILE), NTILE)
                t = mm(d3l[r, :], w2[cols, :], NT) * slope[n, r, :]
                fsum[:, cols] += fold(t)
                dpre[r, cols] = t.astype(BF16)

        partial(4, j, [(dpre, lambda n: w1[n, :], NT)])
        chip_sum(4, j)

    self_forward(0)
    self_forward(1)
    loads[MEMR].wait()
    loads[WCQ].wait()
    project(mem, wcq, 1, None, k2, 0, T)
    project(mem, wcq, 2, cbias_ref[1:2, :], v2, 0, T)
    loads[WCO].wait()
    finish(1, 0, mlow)
    gather(1, 0, mlow)
    cross_forward(0)
    finish(1, 1, mlow)
    gather(1, 1, mlow)
    cross_forward(1)
    loads[W1].wait()
    loads[W2].wait()
    finish(2, 0, slow)
    gather(2, 0, slow)
    ffn_forward(0)
    finish(2, 1, slow)
    gather(2, 1, slow)
    ffn_forward(1)
    cot_copy.wait()
    finish(3, 0, d3l)
    gather(3, 0, d3l)
    ffn_backward(0)
    finish(3, 1, d3l)
    gather(3, 1, d3l)
    ffn_backward(1)
    out_copy = pltpu.make_async_copy(obuf.at[xi], out_hbm, out_sems.at[0])
    out_copy.start()
    for u in range(4):
        grad_rows(u, act, u * R, d3l)
    for u in range(4):
        grad_rows(4 + u, slow, u * R, dpre)
    out_copies = [out_copy]

    def emit(i, src, dst):
        if isinstance(src, tuple):
            u, cols = src
            src = units[u][0].at[pl.ds(units[u][1], R)]
            if cols != slice(None):
                src = units[u][0].at[pl.ds(units[u][1], R), cols]
        c = pltpu.make_async_copy(src, dst, out_sems.at[i])
        c.start()
        out_copies.append(c)

    for u in range(4):
        emit(1 + u, (u, slice(None)), g2_hbm.at[pl.ds(u * R, R)])
        emit(5 + u, (4 + u, slice(None)), g1_hbm.at[pl.ds(u * R, R)])

    def upstream(low, wo, j):
        @pl.loop(0, CH // R)
        def _(i):
            r = pl.ds(pl.multiple_of(j * CH + i * R, R), R)
            up[pl.ds(pl.multiple_of(i * R, R), R), :] = mm(low[r, :], wo[...], NT).astype(BF16)

    dk, dv = slope.at[0], slope.at[1]

    def cross_backward(j):
        upstream(d2l, wco, j)
        attend_back(q2, k2, v2, lse2, j, False, dk, dv, j == 0, 2)
        partial(5, j, [(dql, lambda n: wcq[0, n, :], NT)])
        chip_sum(5, j)

    kT[...] = jnp.transpose(k2[...])
    finish(4, 0, d2l)
    gather(4, 0, d2l)
    cross_backward(0)
    finish(4, 1, d2l)
    gather(4, 1, d2l)
    cross_backward(1)
    finish_back(dk, dv, 2)
    grad_rows(8, c2, 0, d2l)
    grad_cols([(9, dql)], mlow)
    grad_cols([(10, dkl), (11, dvl)], mem)
    emit(9, (8, slice(None)), gco_hbm)
    for u in range(3):
        for b in range(D // R):
            emit(10 + 4 * u + b, (9 + u, pl.ds(b * R, R)), gcq_hbm.at[u, pl.ds(b * R, R)])

    kT[...] = jnp.transpose(k1[...])
    d1l = d3l
    finish(5, 0, d1l)
    finish(5, 1, d1l)
    gather(5, 0, d1l)
    gather(5, 1, d1l)
    for j in range(2):
        partial(6, j, [(dkl, lambda n: wcq[1, n, :], NT), (dvl, lambda n: wcq[2, n, :], NT)])
    scatter_send(6)
    for j in range(2):
        upstream(d1l, wso, j)
        attend_back(q1, k1, v1, lse1, j, True, dk, dv, j == 0, 0)
    scatter_finish(6, None, mem_out := obuf.at[1 - xi])
    emit(22, mem_out, mg_hbm)
    finish_back(dk, dv, 0)
    for j in range(2):
        partial(7, j, [(dql, lambda n: wsq[0, n, :], NT), (dkl, lambda n: wsq[1, n, :], NT),
                       (dvl, lambda n: wsq[2, n, :], NT)])
    scatter_send(7)
    grad_rows(12, c1, 0, d1l)
    grad_cols([(13, dql), (14, dkl), (15, dvl)], xin)
    emit(23, (12, slice(None)), gso_hbm)
    for u in range(3):
        for b in range(D // R):
            emit(24 + 4 * u + b, (13 + u, pl.ds(b * R, R)), gsq_hbm.at[u, pl.ds(b * R, R)])
    out_copy.wait()
    scatter_finish(7, dcur, obuf.at[xi])
    emit(36, obuf.at[xi], ig_hbm)
    small_ref[...] = jnp.zeros_like(small_ref)
    for i in range(9):
        small_ref[i:i + 1, :] = jnp.sum(sums[i], axis=0, keepdims=True)
    small_ref[9:10, :] = jnp.sum(fsum[...], axis=0, keepdims=True)
    for i in range(4):
        small_ref[10:11, i * HC:(i + 1) * HC] = jnp.sum(hsum[i], axis=0, keepdims=True)
    for c in out_copies[1:]:
        c.wait()


def shards(inputs, memory, prefix, self_qkv, self_bias, self_out, cross_qkv, cross_bias, cross_out,
           ffn_in, ffn_in_bias, ffn_out, norm_gain, norm_shift, out_bias, cotangent):
    T, D = inputs.shape
    HC = self_out.shape[0]
    FF = ffn_out.shape[0]
    R = T // 4
    norms = jnp.concatenate(
        [norm_gain.T, norm_shift.T, out_bias.T, jnp.zeros((7, D), BF16)], axis=0).astype(F32)
    sds = jax.ShapeDtypeStruct
    v = pltpu.VMEM
    dma = pltpu.SemaphoreType.DMA
    outs = pl.pallas_call(
        functools.partial(layer_kernel, T, D, HC, FF),
        out_shape=(
            sds((R, D), BF16), sds((R, D), BF16), sds((R, D), BF16),
            sds((3, D, HC), BF16), sds((HC, D), BF16), sds((3, D, HC), BF16), sds((HC, D), BF16),
            sds((D, FF), BF16), sds((FF, D), BF16), sds((16, D), F32),
        ),
        in_specs=[ANY, ANY, SMEM] + [ANY] * 7 + [VMEM] * 4,
        out_specs=(ANY,) * 9 + (VMEM,),
        scratch_shapes=[
            v((T, D), BF16), v((T, D), BF16), v((3, D, HC), BF16), v((HC, D), BF16), v((3, D, HC), BF16),
            v((HC, D), BF16), v((D, FF), BF16), v((FF, D), BF16), v((2, R, D), BF16),
        ] + [v((T, HC), BF16)] * 8 + [v((8, T), F32)] * 2 + [
            v((T, D), BF16), v((T, D), BF16), v((T, D), BF16), v((T, D), BF16),
            v((T, FF), BF16), v((FF // 256, T, 256), F32), v((T, FF), BF16),
            v((2, R, D), F32), v((2, R, D), F32), v((2, R, 128), F32), v((2, R, 128), F32), v((2, R, D), F32),
            v((2, R, D), BF16), v((2, R, D), BF16), v((2, R, D), F32), v((2, R, D), BF16), v((2, 2, R, D), BF16),
            v((T, HC), BF16), v((T, HC), BF16), v((T, HC), BF16), v((HC, T), BF16), v((HC, R), F32),
            v((4 * R, HC), BF16), v((4 * R, HC), BF16), v((T // 2, HC), BF16), v((8 * R, D), BF16),
            v((9, 8, D), F32), v((8, FF), F32), v((4, 8, HC), F32),
            dma((9,)), dma((40,)), dma((8, 2)), dma((8, 2)), dma((8, 2)), dma((8, 2)), dma((8, 2)), dma((8, 2)),
        ],
        compiler_params=pltpu.CompilerParams(
            collective_id=0, has_side_effects=True, vmem_limit_bytes=64 * 2**20 - 256 * 1024),
    )(inputs, memory, prefix, self_qkv, self_out, cross_qkv, cross_out, ffn_in, ffn_out, cotangent,
      norms, self_bias.astype(F32), cross_bias.astype(F32), ffn_in_bias.astype(F32)[None, :])
    out, ig, mg, gsq, gso, gcq, gco, g1, g2, small = outs
    summed = lax.psum((gsq, gso, gcq, gco, g1, g2), "dp")
    gsq, gso, gcq, gco, g1, g2 = [a.astype(F32) for a in summed]
    norm_rows = lax.psum(small[:9], ("dp", "tensor")) * 0.5
    rest = lax.psum(small[9:11], "dp")
    share = D // lax.axis_size("tensor")
    norm_rows = lax.dynamic_slice_in_dim(norm_rows, lax.axis_index("tensor") * share, share, 1).T
    hb = rest[1].reshape(4, HC)
    return (out, ig, mg, gsq, hb[0:2], gso, gcq, hb[2:4], gco, g1, rest[0], g2,
            norm_rows[:, 0:3], norm_rows[:, 3:6], norm_rows[:, 6:9])


def solution(mesh):
    t = "tensor"
    return jax.shard_map(
        shards,
        mesh=mesh,
        in_specs=(
            P("dp", None), P("dp", None), P("dp"), P(None, None, t), P(None, t), P(t, None), P(None, None, t),
            P(None, t), P(t, None), P(None, t), P(t), P(t, None), P(), P(), P(), P(("dp", t), None),
        ),
        out_specs=(
            P(("dp", t), None), P(("dp", t), None), P(("dp", t), None), P(None, None, t), P(None, t), P(t, None),
            P(None, None, t), P(None, t), P(t, None), P(None, t), P(t), P(t, None), P(t, None), P(t, None),
            P(t, None),
        ),
        check_vma=False,
    )
```

time: 1210 us -> 521 us (0.43)
  waiting for transfers between devices: 885 us -> 209 us
  Pallas kernels: 0 us -> 209 us
  matrix products: 168 us -> 0 us
  other arithmetic: 60.3 us -> 18 us
  local copies, waits for them, and re-layouts: 35.2 us -> 5.7 us
  blocking collectives: 37.7 us -> 63.9 us
    psum x1, waiting for transfers between devices: 518 us -> 209 us  [shards(): summed = lax.psum((gsq, gso, gcq, gco, g1, g2), 'dp')]
    reduce_scatter x7 -> x0, waiting for transfers between devices: 234 us -> none  [the longest x1 46.6 us: shards(): lax.psum_scatter(forward_term(self_context, self_out), 'tensor', scatter_...]
    pallas_call x0 -> x1, Pallas kernels: none -> 209 us  [shards(): pl.pallas_call(functools.partial(layer_kernel, T, D, HC, FF), out_shape=(...]
    dot_general x42 -> x0, matrix products: 168 us -> none  [the longest x2 29.4 us: attention_backward(): jnp.einsum('lhe,mhe->hlm', grad_heads, split_heads(values), preferred_ele...]
    all_gather x5 -> x0, waiting for transfers between devices: 84.8 us -> none  [the longest x1 22.7 us: shards(): lax.all_gather(grad_third.astype(jnp.bfloat16), 'tensor', axis=0, tiled=T...]
    unnamed x19 -> x1, waiting for transfers between devices: 47.6 us -> 0.02 us
    unnamed x170 -> x21, local copies, waits for them, and re-layouts: 34.9 us -> 3.21 us
    reduce_sum x14 -> x0, other arithmetic: 30.3 us -> none  [the longest x2 16.5 us: attention_forward(): totals = jnp.sum(weights, axis=-1, keepdims=True)]
  transfers between devices with their start and end apart: 16 -> 1, of which waited for: 14 -> 1; matrix products, arithmetic and copies ran while one was open for 8% -> 0% of each run, Pallas kernels for 0% -> 0%
where the time goes in v1:
time: 521 us; the launch traced here: 520 us
  Pallas kernels  209 us (40%)
  waiting for transfers between devices  209 us (40%)
  blocking collectives  63.9 us (12%)
  other arithmetic  18 us (3%)
  between operations  14.8 us (3%)
  local copies, waits for them, and re-layouts  5.7 us (1%)
    pallas_call x1, Pallas kernels, shards(): pl.pallas_call(functools.partial(layer_kernel, T, D, HC, FF), out_shape=(...  209 us
    psum x1, waiting for transfers between devices, shards(): summed = lax.psum((gsq, gso, gcq, gco, g1, g2), 'dp')  209 us
    psum x1, blocking collectives, shards(): norm_rows = lax.psum(small[:9], ('dp', 'tensor')) * 0.5  41 us
    psum x1, blocking collectives, shards(): rest = lax.psum(small[9:11], 'dp')  22.9 us
    convert_element_type x6, other arithmetic, shards(): gsq, gso, gcq, gco, g1, g2 = [a.astype(F32) for a in summed]  12.7 us
  transfers between devices with their start and end apart: 1, of which 1 were waited for; matrix products, arithmetic and copies ran while one was open for 0% of the time, Pallas kernels for 0%

profile of v1, /device:TPU:0, one launch (start us, length us, event | category | flops | bytes accessed | tf_op | source)
XLA Modules:
  0.0 520.1 jit_solution(8116920132081504394)
XLA Ops:
  7.2 0.0 all-reduce.3.cloned.1.call-start
  7.2 1.3 broadcast_in_dim.11
  8.5 1.3 convert_element_type.29.sbias_ref
  9.8 1.3 convert_element_type.30.cbias_ref
  11.7 0.1 pad.3.clone
  11.8 1.4 maximum_convert_fusion.norm_ref
  13.2 209.0 %shard_map.271 = (bf16[256,1024]{1,0:T(8,128)(2,1)}, bf16[256,1024]{1,0:T(8,128)(2,1)}, bf16[256,1024]{1,0:T(8,128)(2,1)}, bf16[3,1024,256]{2,1,0:T(8,128)(2,1)}...) custom-call(bf16[1024,1024]{1,0:T(8,128)(2,1)} %x_hbm.1, ...), custom_call_target="tpu_custom_call" | custom-call | tf_op jit(solution)/shard_map/pallas_call | solution.py:534
  222.2 0.0 copy-start.8
  222.2 0.0 all-reduce.3.cloned.1.call-update
  222.2 0.8 copy-done.8
  223.0 22.9 %psum.57 = f32[2,1024]{1,0:T(2,128)S(1)} all-reduce(f32[2,1024]{1,0:T(2,128)S(1)} %slice.33), channel_id=1, replica_groups=mesh['dp'=8,'tensor'=4] {'dp'}, use_global_device_ids=true, to_apply=%region_1.0 | all-reduce | flops 2048 | bytes 16384 | tf_op jit(solution)/shard_map/psum | solution.py:564
  245.9 0.6 slice.45
  246.5 0.6 slice.35
  247.1 0.6 slice.37
  247.7 41.0 %psum.63 = f32[9,1024]{1,0:T(8,128)S(1)} all-reduce(f32[9,1024]{1,0:T(8,128)S(1)} %bitcast.8), channel_id=1, replica_groups=mesh['dp'=8,'tensor'=4] {'dp','tensor'}, use_global_device_ids=true, to_apply=%region_7.0 | all-reduce | flops 9216 | bytes 73728 | tf_op jit(solution)/shard_map/psum | solution.py:563
  288.8 0.6 fusion.1
  289.4 208.8 %all-reduce.3.cloned.1.call-done = (bf16[3,1024,256]{2,1,0:T(8,128)(2,1)}, bf16[256,1024]{1,0:T(8,128)(2,1)}, bf16[3,1024,256]{2,1,0:T(8,128)(2,1)}, bf16[256,10...) async-done(((bf16[3,1024,256]{2,1,0:T(8,128)(2,1)}, bf16[256,1024]{1,0:T(8,128)(2,1)}, bf16[3,1024,256]{2,1,0:T(8,128)(2,1)}, ...) | async-done | bytes 8388624 | tf_op jit(solution)/shard_map/psum | solution.py:561
  498.2 4.2 convert_element_type.35
  502.4 0.0 copy-done
  502.4 2.5 convert_element_type.36
  504.9 0.0 copy-done.2
  504.9 1.9 convert_element_type.31
  506.8 0.0 copy-done.1
  506.8 1.9 convert_element_type.33
  508.7 0.0 copy-done.4
  508.7 1.1 convert_element_type.32
  509.8 0.0 copy-done.3
  509.8 1.1 convert_element_type.34
  510.9 0.0 copy-done.7
  510.9 0.8 copy.41
  511.7 0.8 copy.42
  512.5 0.8 copy.43
  (14 shorter events, 0.1 us)
Async XLA Ops:
  7.2 491.0 %all-reduce.3.cloned.1.call-start = ((), (), s32[]{:S(2)}) async-start(), calls=%async_computation | async-start | bytes 16777216 | tf_op jit(solution)/shard_map/psum | solution.py:561
  222.2 0.8 copy-start.8
  498.2 4.2 copy-start
  502.4 2.5 copy-start.2
  504.9 1.9 copy-start.1
  506.8 1.9 copy-start.4
  506.8 3.0 copy-start.3
  508.7 2.2 copy-start.7
  508.7 3.0 copy-start.6
  509.8 2.7 copy-start.5
Sparse Core Ops, SparseCore 0:
  222.3 275.7 all-reduce.2

commit v2 on v1

--- a/solution.py
+++ b/solution.py
@@ -11,6 +11,9 @@
 HEAD_DIM = 64
 EPS = 1e-05
 MASKED = -1e30
+SLOTS = 8
+LAG = (1, 2, 2, 1, 2, 2, 1)
+LAST = (1, 1, 1, 1, 1, 1, 1)
 F32 = jnp.float32
 BF16 = jnp.bfloat16
 MESH = pl.DeviceIdType.MESH
@@ -33,21 +36,20 @@
 def layer_kernel(
     T, D, HC, FF,
     x_hbm, mem_hbm, prefix_ref, wsq_hbm, wso_hbm, wcq_hbm, wco_hbm, w1_hbm, w2_hbm, cot_hbm,
-    norm_ref, sbias_ref, cbias_ref, fbias_ref,
+    norm_ref, sbias_ref, cbias_ref,
     out_hbm, ig_hbm, mg_hbm, gsq_hbm, gso_hbm, gcq_hbm, gco_hbm, g1_hbm, g2_hbm, small_ref,
     xin, mem, wsq, wso, wcq, wco, w1, w2, cot,
     q1, k1, v1, c1, q2, k2, v2, c2, lse1, lse2,
     mlow, slow, d3l, d2l, act, slope, dpre,
     n1, n2, inv1, inv2, dcur,
     chip_send, chip_recv, acc, x_send, x_recv,
-    dql, dkl, dvl, kT, dqT, qm, dom, up, G,
+    dql, dkl, dvl, kT, dqT, qm, dom, up, ring, sring,
     sums, fsum, hsum,
-    in_sems, out_sems, cs_sem, cr_sem, xs_sem, xr_sem, as_sem, ar_sem,
+    in_sems, out_sems, cs_sem, cr_sem, xs_sem, xr_sem, as_sem, ar_sem, ds_sem, dr_sem, do_sem, ss_sem, sr_sem,
 ):
     H = HC // HEAD_DIM
     obuf = cot
-    units = [(G, u * (T // 4)) for u in range(8)] + [(slow, u * (T // 4)) for u in range(4)] + [
-        (w1, u * (T // 4)) for u in range(4)]
+    units = [(ref, u * (T // 4)) for ref in (xin, w2, slow, w1) for u in range(4)]
     CH = T // 2
     R = T // 4
     dp = lax.axis_index("dp")
@@ -56,21 +58,36 @@
     ci = lax.rem(tn, 2)
     mate = (dp, xi * 2 + (1 - ci))
     peer = (dp, (1 - xi) * 2 + ci)
+    yi = lax.rem(dp, 2)
+    zi = lax.rem(dp // 2, 4)
+    inner = (zi == 1) | (zi == 2)
+    outer = jnp.logical_not(inner)
+    ymate = (dp + 1 - 2 * yi, tn)
+    zmate = (dp + 2 - 4 * lax.rem(zi, 2), tn)
+    across = (dp + 6 - 4 * zi, tn)
 
     srcs = [(x_hbm, xin), (wsq_hbm, wsq), (wso_hbm, wso), (mem_hbm, mem), (wcq_hbm, wcq), (wco_hbm, wco),
             (w1_hbm, w1), (w2_hbm, w2)]
     loads = [pltpu.make_async_copy(a, b, in_sems.at[i]) for i, (a, b) in enumerate(srcs)]
     loads.append(pltpu.make_async_copy(cot_hbm, cot.at[xi], in_sems.at[len(srcs)]))
-    for load in loads:
-        load.start()
     XIN, WSQ, WSO, MEMR, WCQ, WCO, W1, W2, COT = range(9)
-
+    loads[COT].start()
     barrier = pltpu.get_barrier_semaphore()
-    for other in (mate, peer):
+    for other in (mate, peer, ymate, zmate):
         pl.semaphore_signal(barrier, inc=1, device_id=other, device_id_type=MESH)
-    pl.semaphore_wait(barrier, 2)
-
     loads[COT].wait()
+    for i in (XIN, WSQ):
+        loads[i].start()
+
+    @pl.when(inner)
+    def _():
+        pl.semaphore_signal(barrier, inc=1, device_id=across, device_id_type=MESH)
+        pl.semaphore_wait(barrier, 5)
+
+    @pl.when(outer)
+    def _():
+        pl.semaphore_wait(barrier, 4)
+
     cot_copy = pltpu.make_async_remote_copy(
         src_ref=cot.at[xi], dst_ref=cot.at[xi], send_sem=xs_sem.at[0, 0], recv_sem=xr_sem.at[0, 0],
         device_id=peer, device_id_type=MESH)
@@ -91,12 +108,12 @@
         return jnp.where(lane // HEAD_DIM == h, 1.0, 0.0)[0:1].astype(BF16)
 
     def project(src, w, wi, bias, dst, r0, n, scale=None):
-        @pl.loop(0, n // R)
+        @pl.loop(0, n // R, unroll=True)
         def _(i):
             r = pl.multiple_of(r0 + i * R, R)
             y = mm(src[pl.ds(r, R), :], w[wi])
             if bias is not None:
-                y = y + bias
+                y = y + bias.astype(F32)
             y = y.astype(BF16)
             if scale is not None:
                 y = y * jnp.asarray(scale, BF16)
@@ -146,7 +163,7 @@
             nk = max(T // 2, r0 + R) if causal else T
             rows = slice(r0, r0 + R)
 
-            @pl.loop(0, H)
+            @pl.loop(0, H, unroll=4)
             def _(h):
                 m = head_mask(h)
                 qh = q[rows, :] * m
@@ -166,7 +183,7 @@
                 hr = pl.ds(pl.multiple_of(h * HEAD_DIM, HEAD_DIM), HEAD_DIM)
                 dqT[hr, :] = mm(kT[hr, :nk], ds)
 
-            @pl.loop(0, nk // R)
+            @pl.loop(0, nk // R, unroll=True)
             def _(kt):
                 kr = pl.ds(pl.multiple_of(kt * R, R), R)
                 a = mm(pbuf[kr, :], dom[...])
@@ -184,6 +201,7 @@
             dq = jnp.transpose(dqT[...]) * SC
             hsum[slot] += fold(dq)
             dql[rows, :] = dq.astype(BF16)
+            tick()
 
     def finish_back(dk, dv, slot):
         @pl.loop(0, T // R)
@@ -194,10 +212,16 @@
             dvl[r, :] = a.astype(BF16)
             dkl[r, :] = dk[r, :].astype(BF16)
 
+    def sent(s, j):
+        return d2l.at[pl.ds(j * R, R)] if s > 5 else chip_send
+
+    def kept(s, j):
+        return n2.at[j] if s > 5 else acc
+
     def chip_copy(s, j):
         dst = mlow.at[pl.ds(j * R, R)] if s == 7 else chip_recv.at[j]
         return pltpu.make_async_remote_copy(
-            src_ref=chip_send.at[j], dst_ref=dst, send_sem=cs_sem.at[s, j], recv_sem=cr_sem.at[s, j],
+            src_ref=sent(s, j), dst_ref=dst, send_sem=cs_sem.at[s, j], recv_sem=cr_sem.at[s, j],
             device_id=mate, device_id_type=MESH)
 
     def x_copy(s, j):
@@ -211,9 +235,11 @@
             src_ref=low.at[rows], dst_ref=low.at[rows], send_sem=as_sem.at[s, j], recv_sem=ar_sem.at[s, j],
             device_id=mate, device_id_type=MESH)
 
-    NTILE = 256
+    NTILE = 1024
 
     def partial(s, j, terms):
+        send, own = sent(s, j), kept(s, j)
+
         def tile(r, n):
             y = None
             for lhs, rhs, dims in terms:
@@ -224,24 +250,24 @@
         @pl.loop(0, D // NTILE)
         def _(n):
             n = pl.ds(pl.multiple_of(n * NTILE, NTILE), NTILE)
-            chip_send[j, :, n] = tile(mates(j), n).astype(BF16)
+            send[:, n] = tile(mates(j), n).astype(BF16)
 
         chip_copy(s, j).start()
 
         @pl.loop(0, D // NTILE)
         def _(n):
             n = pl.ds(pl.multiple_of(n * NTILE, NTILE), NTILE)
-            acc[j, :, n] = tile(mine(j), n)
+            own[:, n] = tile(mine(j), n)
 
     RT = 32
 
     def chip_sum(s, j):
         chip_copy(s, j).wait()
 
-        @pl.loop(0, R // RT)
+        @pl.loop(0, R // RT, unroll=2)
         def _(i):
             r = pl.ds(pl.multiple_of(i * RT, RT), RT)
-            x_send[j, r, :] = (acc[j, r, :] + chip_recv[j, r, :].astype(F32)).astype(BF16)
+            x_send[j, r, :] = (acc[r, :] + chip_recv[j, r, :].astype(F32)).astype(BF16)
 
         x_copy(s, j).start()
 
@@ -274,7 +300,7 @@
         x_copy(s, j).wait()
         base = mine(j)
 
-        @pl.loop(0, R // RT)
+        @pl.loop(0, R // RT, unroll=2)
         def _(i):
             r = pl.ds(pl.multiple_of(i * RT, RT), RT)
             g = pl.ds(pl.multiple_of(base + i * RT, RT), RT)
@@ -320,20 +346,20 @@
             chip_copy(s, j).wait()
         j = 1 - xi
 
-        @pl.loop(0, R // RT)
+        @pl.loop(0, R // RT, unroll=2)
         def _(i):
             r = pl.ds(pl.multiple_of(i * RT, RT), RT)
-            x_send[0, r, :] = (acc[j, r, :] + got(s, j, i)).astype(BF16)
+            x_send[0, r, :] = (n2[j, r, :] + got(s, j, i)).astype(BF16)
 
         x_copy(s, 0).start()
 
     def scatter_finish(s, extra, dst):
         x_copy(s, 0).wait()
 
-        @pl.loop(0, R // RT)
+        @pl.loop(0, R // RT, unroll=2)
         def _(i):
             r = pl.ds(pl.multiple_of(i * RT, RT), RT)
-            t = acc[xi, r, :] + got(s, xi, i) + x_recv[s % 2, 0, r, :].astype(F32)
+            t = n2[xi, r, :] + got(s, xi, i) + x_recv[s % 2, 0, r, :].astype(F32)
             if extra is not None:
                 t = t + extra[xi, r, :]
             dst[r, :] = t.astype(BF16)
@@ -346,15 +372,282 @@
             unit[r0:r0 + R, n] = mm(lhs[:, pl.ds(c0, R)], rhs[:, n], TN).astype(BF16)
 
     def grad_cols(pairs, lhs):
-        @pl.loop(0, D // R)
+        @pl.loop(0, D // R, unroll=True)
         def _(b):
             cols = pl.ds(pl.multiple_of(b * R, R), R)
             for u, rhs in pairs:
                 unit, r0 = units[u]
                 unit[r0:r0 + R, cols] = mm(lhs[:, cols], rhs[...], TN).astype(BF16)
 
+
+    Q = R // 4
+
+    def ring_rows(u, at, n=Q):
+        return ring.at[pl.ds((u % SLOTS) * 8 * Q + at * Q, n)]
+
+    def hop(u, i):
+        ref, r0 = units[u]
+        k = u % SLOTS
+
+        def rows(at):
+            return ref.at[pl.ds(pl.multiple_of(r0 + at * Q, Q), Q)]
+
+        hz = zi // 2
+        if i == "a1":
+            n, src, dst, dev = 0, rows(1 - yi), ring_rows(u, 0), ymate
+        elif i == "a2":
+            n, src, dst, dev = 1, rows(yi), ring_rows(u, 1), zmate
+        elif i == "a3":
+            n, src, dst, dev = 2, rows(yi), ring_rows(u, 7), across
+        elif i == "a4":
+            n, src, dst, dev = 3, rows(yi), ring_rows(u, 1), zmate
+        elif i == "a5i":
+            n, src, dst, dev = 4, rows(yi), ring_rows(u, 2), ymate
+        elif i == "a5o":
+            n, src, dst, dev = 4, ring_rows(u, 1), ring_rows(u, 2), ymate
+        elif i == "b1":
+            n, src, dst, dev = 5, ref.at[pl.ds(r0 + 2 * Q, 2 * Q)], ring_rows(u, 6, 2 * Q), zmate
+        elif i == "b2":
+            n, src, dst, dev = 6, rows(2 + 1 - hz), ring_rows(u, 3), across
+        elif i == "b3":
+            n, src, dst, dev = 7, rows(2 + hz), ring_rows(u, 4), ymate
+        elif i == "b4":
+            n, src, dst, dev = 8, rows(2 + hz), ring_rows(u, 5), across
+        elif i == "b5o":
+            n, src, dev = 9, rows(2 + hz), zmate
+            dst = ring.at[pl.ds(pl.multiple_of(k * 8 * Q + (6 + hz) * Q, Q), Q)]
+        elif i == "b5t":
+            n, src, dev = 10, ring_rows(u, 5), zmate
+            dst = ring.at[pl.ds(pl.multiple_of(k * 8 * Q + (7 - hz) * Q, Q), Q)]
+        return pltpu.make_async_remote_copy(
+            src_ref=src, dst_ref=dst, send_sem=ds_sem.at[k, n], recv_sem=dr_sem.at[k, n],
+            device_id=dev, device_id_type=MESH)
+
+    def add(u, row, at, n):
+        ref, r0 = units[u]
+        base = (u % SLOTS) * 8 * Q + at * Q
+
+        @pl.loop(0, n // 16)
+        def _(i):
+            a = pl.ds(pl.multiple_of(r0 + row * Q + i * 16, 16), 16)
+            b = pl.ds(pl.multiple_of(base + i * 16, 16), 16)
+            ref[a, :] = (ref[a, :].astype(F32) + ring[b, :].astype(F32)).astype(BF16)
+
+    def store(u, i, src, row, n=Q):
+        sem = do_sem.at[u % SLOTS, i]
+
+        def rows(base):
+            return pl.ds(pl.multiple_of(base + row * Q, Q), n)
+
+        if u < 8:
+            whole = (g2_hbm if u < 4 else g1_hbm).at[rows(u % 4 * R)]
+        elif u % 4 == 0:
+            whole = (gco_hbm if u == 8 else gso_hbm).at[rows(0)]
+        else:
+            dst = (gcq_hbm if u < 12 else gsq_hbm).at[u % 4 - 1]
+            return [pltpu.make_async_copy(src.at[:, pl.ds(b * R, R)], dst.at[rows(b * R)], do_sem.at[u % SLOTS, 4 * b + i])
+                    for b in range(D // R)]
+        return [pltpu.make_async_copy(src, whole, sem)]
+
+    def stores(u):
+        ref, r0 = units[u]
+        hz = zi // 2
+
+        def rows(at):
+            return ref.at[pl.ds(pl.multiple_of(r0 + at * Q, Q), Q)]
+
+        both = store(u, 0, ring_rows(u, 2), 1 - yi)
+        if_inner = store(u, 1, rows(yi), yi) + store(u, 2, rows(2 + hz), 2 + hz) + store(u, 3, ring_rows(u, 5), 3 - hz)
+        if_outer = store(u, 1, ring_rows(u, 1), yi) + store(u, 2, ring_rows(u, 6, 2 * Q), 2, 2 * Q)
+        return both, if_inner, if_outer
+
+    def advance(u, stage):
+        hz = zi // 2
+        if stage == 0:
+            hop(u, "a1").start()
+
+            @pl.when(outer)
+            def _():
+                hop(u, "b1").start()
+        elif stage == 1:
+            hop(u, "a1").wait()
+            add(u, yi, 0, Q)
+
+            @pl.when(outer)
+            def _():
+                hop(u, "a2").start()
+                hop(u, "b1").wait_send()
+
+            @pl.when(inner)
+            def _():
+                hop(u, "b1").wait_recv()
+                add(u, 2, 6, 2 * Q)
+                hop(u, "b2").start()
+        elif stage == 2:
+            @pl.when(outer)
+            def _():
+                hop(u, "a2").wait_send()
+
+            @pl.when(inner)
+            def _():
+                hop(u, "b2").wait()
+                add(u, 2 + hz, 3, Q)
+                hop(u, "b3").start()
+                hop(u, "a2").wait_recv()
+                add(u, yi, 1, Q)
+                hop(u, "a3").start()
+        elif stage == 3:
+            @pl.when(inner)
+            def _():
+                hop(u, "a3").wait()
+                add(u, yi, 7, Q)
+                hop(u, "a4").start()
+                hop(u, "a5i").start()
+                hop(u, "b3").wait()
+                add(u, 2 + hz, 4, Q)
+                hop(u, "b4").start()
+                hop(u, "b5o").start()
+        elif stage == 4:
+            @pl.when(inner)
+            def _():
+                hop(u, "b4").wait()
+                hop(u, "b5t").start()
+
+            @pl.when(outer)
+            def _():
+                hop(u, "a4").wait_recv()
+                hop(u, "a5o").start()
+        elif stage == 5:
+            both, if_inner, if_outer = stores(u)
+
+            @pl.when(inner)
+            def _():
+                hop(u, "a5i").wait()
+                for c in if_inner:
+                    c.start()
+
+            @pl.when(outer)
+            def _():
+                hop(u, "a5o").wait()
+                hop(u, "b5o").wait_recv()
+                hop(u, "b5t").wait_recv()
+                for c in if_outer:
+                    c.start()
+
+            for c in both:
+                c.start()
+        else:
+            both, if_inner, if_outer = stores(u)
+            for c in both:
+                c.wait()
+
+            @pl.when(inner)
+            def _():
+                for i in ("a4", "b5o", "b5t"):
+                    hop(u, i).wait_send()
+                for c in if_inner:
+                    c.wait()
+
+            @pl.when(outer)
+            def _():
+                for c in if_outer:
+                    c.wait()
+
+    def small_hop(i):
+        dev = (mate, ymate, zmate, across, zmate)[i]
+        return pltpu.make_async_remote_copy(
+            src_ref=small_ref, dst_ref=sring.at[2 if i == 4 else i], send_sem=ss_sem.at[i],
+            recv_sem=sr_sem.at[i], device_id=dev, device_id_type=MESH)
+
+    def advance_small(stage):
+        if stage == 0:
+            for i in range(9):
+                small_ref[i:i + 1, :] = jnp.sum(sums[i], axis=0, keepdims=True)
+            small_ref[9:10, :] = jnp.sum(fsum[...], axis=0, keepdims=True)
+            for i in range(4):
+                small_ref[10:11, i * HC:(i + 1) * HC] = jnp.sum(hsum[i], axis=0, keepdims=True)
+            small_ref[11:16, :] = jnp.zeros((5, D), F32)
+            small_hop(0).start()
+        elif stage == 1:
+            small_hop(0).wait()
+            small_ref[0:9, :] += sring[0, 0:9, :]
+            small_hop(1).start()
+        elif stage == 2:
+            small_hop(1).wait()
+            small_ref[...] += sring[1]
+
+            @pl.when(outer)
+            def _():
+                small_hop(2).start()
+        elif stage == 3:
+            @pl.when(outer)
+            def _():
+                small_hop(2).wait_send()
+
+            @pl.when(inner)
+            def _():
+                small_hop(2).wait_recv()
+                small_ref[...] += sring[2]
+                small_hop(3).start()
+        elif stage == 4:
+            @pl.when(inner)
+            def _():
+                small_hop(3).wait()
+                small_ref[...] += sring[3]
+                small_hop(4).start()
+        elif stage == 5:
+            @pl.when(inner)
+            def _():
+                small_hop(4).wait_send()
+
+            @pl.when(outer)
+            def _():
+                small_hop(4).wait_recv()
+                small_ref[...] = sring[2]
+
+    ready, flight, lag = [], [], list(LAG)
+
+    def launch(n=1):
+        new = []
+        while n and ready and (ready[0] == "small" or len(flight) + len(new) < SLOTS):
+            u = ready.pop(0)
+            if u == "small":
+                advance_small(0)
+            else:
+                advance(u, 0)
+            new.append([u, 1, lag[1]])
+            n -= 1
+        return new
+
+    def start(n=1):
+        flight.extend(launch(n))
+
+    def step(item):
+        item[2] -= 1
+        if item[2] > 0:
+            return
+        if item[0] == "small":
+            advance_small(item[1])
+        else:
+            advance(item[0], item[1])
+        item[1] += 1
+        item[2] = lag[item[1] % 7]
+
+    def tick(n=1):
+        for item in [i for i in flight if i[1] == 6]:
+            step(item)
+            if item[1] == 7:
+                flight.remove(item)
+        new = launch(n)
+        for item in flight:
+            if item[1] < 6:
+                step(item)
+        flight.extend(new)
+
     loads[XIN].wait()
     loads[WSQ].wait()
+    for i in (WSO, MEMR, WCQ, WCO, W1, W2):
+        loads[i].start()
     project(xin, wsq, 0, sbias_ref[0:1, :], q1, 0, T, SC)
     project(xin, wsq, 1, None, k1, 0, T)
     project(xin, wsq, 2, sbias_ref[1:2, :], v1, 0, T)
@@ -376,10 +669,10 @@
         def _(i):
             r = pl.ds(pl.multiple_of(j * CH + i * R, R), R)
 
-            @pl.loop(0, FF // NTILE)
+            @pl.loop(0, FF // 256, unroll=4)
             def _(n):
-                cols = pl.ds(pl.multiple_of(n * NTILE, NTILE), NTILE)
-                pre = mm(slow[r, :], w1[:, cols]) + fbias_ref[:, cols]
+                cols = pl.ds(pl.multiple_of(n * 256, 256), 256)
+                pre = mm(slow[r, :], w1[:, cols]) + norm_ref[9:10, cols]
                 half = 0.5 * (1.0 + lax.erf(pre * (1.0 / math.sqrt(2.0))))
                 act[r, cols] = (pre * half).astype(BF16)
                 slope[n, r, :] = half + pre * jnp.exp(-0.5 * pre * pre) * (1.0 / math.sqrt(2.0 * math.pi))
@@ -392,9 +685,9 @@
         def _(i):
             r = pl.ds(pl.multiple_of(j * CH + i * R, R), R)
 
-            @pl.loop(0, FF // NTILE)
+            @pl.loop(0, FF // 256, unroll=4)
             def _(n):
-                cols = pl.ds(pl.multiple_of(n * NTILE, NTILE), NTILE)
+                cols = pl.ds(pl.multiple_of(n * 256, 256), 256)
                 t = mm(d3l[r, :], w2[cols, :], NT) * slope[n, r, :]
                 fsum[:, cols] += fold(t)
                 dpre[r, cols] = t.astype(BF16)
@@ -429,31 +722,31 @@
     ffn_backward(0)
     finish(3, 1, d3l)
     gather(3, 1, d3l)
+    for u in range(2):
+        grad_rows(u, act, u * R, d3l)
+        ready.append(u)
+        if u == 0:
+            start()
     ffn_backward(1)
     out_copy = pltpu.make_async_copy(obuf.at[xi], out_hbm, out_sems.at[0])
     out_copy.start()
-    for u in range(4):
+    tick()
+    for u in range(2, 4):
         grad_rows(u, act, u * R, d3l)
+        ready.append(u)
     for u in range(4):
         grad_rows(4 + u, slow, u * R, dpre)
+        ready.append(4 + u)
+    tick()
     out_copies = [out_copy]
 
     def emit(i, src, dst):
-        if isinstance(src, tuple):
-            u, cols = src
-            src = units[u][0].at[pl.ds(units[u][1], R)]
-            if cols != slice(None):
-                src = units[u][0].at[pl.ds(units[u][1], R), cols]
         c = pltpu.make_async_copy(src, dst, out_sems.at[i])
         c.start()
         out_copies.append(c)
 
-    for u in range(4):
-        emit(1 + u, (u, slice(None)), g2_hbm.at[pl.ds(u * R, R)])
-        emit(5 + u, (4 + u, slice(None)), g1_hbm.at[pl.ds(u * R, R)])
-
     def upstream(low, wo, j):
-        @pl.loop(0, CH // R)
+        @pl.loop(0, CH // R, unroll=True)
         def _(i):
             r = pl.ds(pl.multiple_of(j * CH + i * R, R), R)
             up[pl.ds(pl.multiple_of(i * R, R), R), :] = mm(low[r, :], wo[...], NT).astype(BF16)
@@ -464,58 +757,68 @@
         upstream(d2l, wco, j)
         attend_back(q2, k2, v2, lse2, j, False, dk, dv, j == 0, 2)
         partial(5, j, [(dql, lambda n: wcq[0, n, :], NT)])
+        tick()
         chip_sum(5, j)
+
+    def self_backward(j):
+        upstream(d1l, wso, j)
+        attend_back(q1, k1, v1, lse1, j, True, dk, dv, j == 0, 0)
 
     kT[...] = jnp.transpose(k2[...])
     finish(4, 0, d2l)
+    tick()
     gather(4, 0, d2l)
     cross_backward(0)
     finish(4, 1, d2l)
+    tick()
     gather(4, 1, d2l)
+    grad_rows(8, c2, 0, d2l)
+    ready.append(8)
     cross_backward(1)
     finish_back(dk, dv, 2)
-    grad_rows(8, c2, 0, d2l)
     grad_cols([(9, dql)], mlow)
     grad_cols([(10, dkl), (11, dvl)], mem)
-    emit(9, (8, slice(None)), gco_hbm)
-    for u in range(3):
-        for b in range(D // R):
-            emit(10 + 4 * u + b, (9 + u, pl.ds(b * R, R)), gcq_hbm.at[u, pl.ds(b * R, R)])
+    x_again = pltpu.make_async_copy(x_hbm, mem, in_sems.at[0])
+    x_again.start()
+    ready.extend([9, 10, 11])
+    tick()
 
     kT[...] = jnp.transpose(k1[...])
     d1l = d3l
     finish(5, 0, d1l)
+    tick()
+    gather(5, 0, d1l)
+    self_backward(0)
     finish(5, 1, d1l)
-    gather(5, 0, d1l)
+    tick()
     gather(5, 1, d1l)
+    grad_rows(12, c1, 0, d1l)
+    ready.append(12)
     for j in range(2):
         partial(6, j, [(dkl, lambda n: wcq[1, n, :], NT), (dvl, lambda n: wcq[2, n, :], NT)])
+    tick()
     scatter_send(6)
-    for j in range(2):
-        upstream(d1l, wso, j)
-        attend_back(q1, k1, v1, lse1, j, True, dk, dv, j == 0, 0)
+    self_backward(1)
     scatter_finish(6, None, mem_out := obuf.at[1 - xi])
-    emit(22, mem_out, mg_hbm)
+    emit(1, mem_out, mg_hbm)
     finish_back(dk, dv, 0)
+    x_again.wait()
+    grad_cols([(13, dql), (14, dkl), (15, dvl)], mem)
+    ready.extend([13, 14, 15, "small"])
+    lag[:] = LAST
+    tick()
     for j in range(2):
         partial(7, j, [(dql, lambda n: wsq[0, n, :], NT), (dkl, lambda n: wsq[1, n, :], NT),
                        (dvl, lambda n: wsq[2, n, :], NT)])
+    tick()
     scatter_send(7)
-    grad_rows(12, c1, 0, d1l)
-    grad_cols([(13, dql), (14, dkl), (15, dvl)], xin)
-    emit(23, (12, slice(None)), gso_hbm)
-    for u in range(3):
-        for b in range(D // R):
-            emit(24 + 4 * u + b, (13 + u, pl.ds(b * R, R)), gsq_hbm.at[u, pl.ds(b * R, R)])
+    for _ in range(4):
+        tick()
     out_copy.wait()
     scatter_finish(7, dcur, obuf.at[xi])
-    emit(36, obuf.at[xi], ig_hbm)
-    small_ref[...] = jnp.zeros_like(small_ref)
-    for i in range(9):
-        small_ref[i:i + 1, :] = jnp.sum(sums[i], axis=0, keepdims=True)
-    small_ref[9:10, :] = jnp.sum(fsum[...], axis=0, keepdims=True)
-    for i in range(4):
-        small_ref[10:11, i * HC:(i + 1) * HC] = jnp.sum(hsum[i], axis=0, keepdims=True)
+    emit(2, obuf.at[xi], ig_hbm)
+    while ready or flight:
+        tick()
     for c in out_copies[1:]:
         c.wait()
 
@@ -527,7 +830,7 @@
     FF = ffn_out.shape[0]
     R = T // 4
     norms = jnp.concatenate(
-        [norm_gain.T, norm_shift.T, out_bias.T, jnp.zeros((7, D), BF16)], axis=0).astype(F32)
+        [norm_gain.T, norm_shift.T, out_bias.T, ffn_in_bias[None, :], jnp.zeros((6, D), BF16)], axis=0).astype(F32)
     sds = jax.ShapeDtypeStruct
     v = pltpu.VMEM
     dma = pltpu.SemaphoreType.DMA
@@ -538,7 +841,7 @@
             sds((3, D, HC), BF16), sds((HC, D), BF16), sds((3, D, HC), BF16), sds((HC, D), BF16),
             sds((D, FF), BF16), sds((FF, D), BF16), sds((16, D), F32),
         ),
-        in_specs=[ANY, ANY, SMEM] + [ANY] * 7 + [VMEM] * 4,
+        in_specs=[ANY, ANY, SMEM] + [ANY] * 7 + [VMEM] * 3,
         out_specs=(ANY,) * 9 + (VMEM,),
         scratch_shapes=[
             v((T, D), BF16), v((T, D), BF16), v((3, D, HC), BF16), v((HC, D), BF16), v((3, D, HC), BF16),
@@ -547,26 +850,29 @@
             v((T, D), BF16), v((T, D), BF16), v((T, D), BF16), v((T, D), BF16),
             v((T, FF), BF16), v((FF // 256, T, 256), F32), v((T, FF), BF16),
             v((2, R, D), F32), v((2, R, D), F32), v((2, R, 128), F32), v((2, R, 128), F32), v((2, R, D), F32),
-            v((2, R, D), BF16), v((2, R, D), BF16), v((2, R, D), F32), v((2, R, D), BF16), v((2, 2, R, D), BF16),
+            v((R, D), BF16), v((2, R, D), BF16), v((R, D), F32), v((2, R, D), BF16), v((2, 2, R, D), BF16),
             v((T, HC), BF16), v((T, HC), BF16), v((T, HC), BF16), v((HC, T), BF16), v((HC, R), F32),
-            v((4 * R, HC), BF16), v((4 * R, HC), BF16), v((T // 2, HC), BF16), v((8 * R, D), BF16),
+            v((4 * R, HC), BF16), v((4 * R, HC), BF16), v((T // 2, HC), BF16), v((SLOTS * 2 * R, D), BF16), v((4, 16, D), F32),
             v((9, 8, D), F32), v((8, FF), F32), v((4, 8, HC), F32),
-            dma((9,)), dma((40,)), dma((8, 2)), dma((8, 2)), dma((8, 2)), dma((8, 2)), dma((8, 2)), dma((8, 2)),
+            dma((9,)), dma((4,)), dma((8, 2)), dma((8, 2)), dma((8, 2)), dma((8, 2)), dma((8, 2)), dma((8, 2)),
+            dma((SLOTS, 11)), dma((SLOTS, 11)), dma((SLOTS, 16)), dma((5,)), dma((5,)),
         ],
         compiler_params=pltpu.CompilerParams(
             collective_id=0, has_side_effects=True, vmem_limit_bytes=64 * 2**20 - 256 * 1024),
     )(inputs, memory, prefix, self_qkv, self_out, cross_qkv, cross_out, ffn_in, ffn_out, cotangent,
-      norms, self_bias.astype(F32), cross_bias.astype(F32), ffn_in_bias.astype(F32)[None, :])
-    out, ig, mg, gsq, gso, gcq, gco, g1, g2, small = outs
-    summed = lax.psum((gsq, gso, gcq, gco, g1, g2), "dp")
-    gsq, gso, gcq, gco, g1, g2 = [a.astype(F32) for a in summed]
-    norm_rows = lax.psum(small[:9], ("dp", "tensor")) * 0.5
-    rest = lax.psum(small[9:11], "dp")
+      norms, self_bias, cross_bias)
+    out, ig, mg = outs[:3]
+    grads, small = outs[3:9], outs[9]
+    count = lax.axis_size("dp")
+    if count > 8:
+        same = [[g * 8 + i for g in range(count // 8)] for i in range(8)]
+        grads, small = lax.psum((grads, small), "dp", axis_index_groups=same)
+    gsq, gso, gcq, gco, g1, g2 = [g.astype(F32) for g in grads]
     share = D // lax.axis_size("tensor")
-    norm_rows = lax.dynamic_slice_in_dim(norm_rows, lax.axis_index("tensor") * share, share, 1).T
-    hb = rest[1].reshape(4, HC)
-    return (out, ig, mg, gsq, hb[0:2], gso, gcq, hb[2:4], gco, g1, rest[0], g2,
-            norm_rows[:, 0:3], norm_rows[:, 3:6], norm_rows[:, 6:9])
+    rows = lax.dynamic_slice_in_dim(small[:9], lax.axis_index("tensor") * share, share, 1).T
+    hb = small[10].reshape(4, HC)
+    return (out, ig, mg, gsq, hb[0:2], gso, gcq, hb[2:4], gco, g1, small[9], g2,
+            rows[:, 0:3], rows[:, 3:6], rows[:, 6:9])
 
 
 def solution(mesh):

time: 521 us -> 294 us (0.56)
  waiting for transfers between devices: 209 us -> 0 us
  blocking collectives: 63.9 us -> 0 us
  Pallas kernels: 209 us -> 266 us
  between operations: 14.8 us -> 1.51 us
    psum x1 -> x0, waiting for transfers between devices: 209 us -> none  [shards(): summed = lax.psum((gsq, gso, gcq, gco, g1, g2), 'dp')]
    psum x2 -> x0, blocking collectives: 63.9 us -> none  [the longest x1 41 us: shards(): norm_rows = lax.psum(small[:9], ('dp', 'tensor')) * 0.5]
    pallas_call x1, Pallas kernels: 209 us -> 266 us  [shards(): pl.pallas_call(functools.partial(layer_kernel, T, D, HC, FF), out_shape=(...]
    convert_element_type x9 -> x7, other arithmetic: 16.7 us -> 13.4 us  [the longest x6 12.7 us: shards(): gsq, gso, gcq, gco, g1, g2 = [g.astype(F32) for g in grads]]
  transfers between devices with their start and end apart: 1 -> 0, of which waited for: 1 -> 0; matrix products, arithmetic and copies ran while one was open for 0% -> 0% of each run, Pallas kernels for 0% -> 0%
where the time goes in v2:
time: 294 us; the launch traced here: 290 us
  Pallas kernels  266 us (90%)
  other arithmetic  13.4 us (5%)
  local copies, waits for them, and re-layouts  9.29 us (3%)
    pallas_call x1, Pallas kernels, shards(): pl.pallas_call(functools.partial(layer_kernel, T, D, HC, FF), out_shape=(...  266 us
    convert_element_type x6, other arithmetic, shards(): gsq, gso, gcq, gco, g1, g2 = [g.astype(F32) for g in grads]  12.7 us

profile of v2, /device:TPU:0, one launch (start us, length us, event | category | flops | bytes accessed | tf_op | source)
XLA Modules:
  0.0 290.1 jit_solution(17190771853609188206)
XLA Ops:
  0.6 0.7 broadcast_in_dim.6
  1.3 1.6 concatenate.3
  2.9 0.6 convert_element_type.21.norm_ref
  4.2 265.9 %shard_map.271 = (bf16[256,1024]{1,0:T(8,128)(2,1)}, bf16[256,1024]{1,0:T(8,128)(2,1)}, bf16[256,1024]{1,0:T(8,128)(2,1)}, bf16[3,1024,256]{2,1,0:T(8,128)(2,1)}...) custom-call(bf16[1024,1024]{1,0:T(8,128)(2,1)} %x_hbm.1, ...), custom_call_target="tpu_custom_call" | custom-call | tf_op jit(solution)/shard_map/pallas_call | solution.py:837
  270.1 0.7 dynamic-slice_bitcast_fusion
  270.8 0.6 fusion
  271.4 0.8 slice_reduce_fusion
  272.2 0.6 slice.31
  272.8 0.6 slice.33
  273.4 1.4 slice.34
  274.7 0.0 copy-start
  274.7 4.2 %convert_element_type.26 = f32[1024,1024]{1,0:T(8,128)} convert(bf16[1024,1024]{1,0:T(8,128)(2,1)} %get-tuple-element.33) | non-fusion elementwise | flops 1048576 | bytes 6291456 | tf_op jit(solution)/shard_map/convert_element_type | solution.py:870
  278.9 0.0 copy-done
  278.9 0.0 copy-start.2
  278.9 2.5 convert_element_type.27
  281.4 0.0 copy-done.2
  281.4 0.0 copy-start.1
  281.4 1.9 convert_element_type.22
  283.4 0.0 copy-done.1
  283.4 0.0 copy-start.4
  283.4 0.0 copy-start.3
  283.4 1.9 convert_element_type.24
  285.3 0.0 copy-done.4
  285.3 1.1 convert_element_type.23
  286.4 0.0 copy-done.3
  286.4 1.1 convert_element_type.25
  287.5 0.0 copy-done.7
  287.5 0.8 copy.35
  288.3 0.0 copy-done.6
  288.3 0.8 copy.36
  289.1 0.0 copy-done.5
  289.1 0.8 copy.37
  (4 shorter events, 0.0 us)
Async XLA Ops:
  274.7 4.2 %copy-start = (bf16[1024,1024]{1,0:T(8,128)(2,1)S(1)}, bf16[1024,1024]{1,0:T(8,128)(2,1)}, u32[]{:S(2)}) copy-start(bf16[1024,1024]{1,0:T(8,128)(2,1)} %get-tuple-element.34) | copy-start | bytes 6291460
  278.9 2.5 copy-start.2
  281.4 1.9 copy-start.1
  283.4 1.9 copy-start.4
  283.4 3.0 %copy-start.3 = (bf16[256,1024]{1,0:T(8,128)(2,1)S(1)}, bf16[256,1024]{1,0:T(8,128)(2,1)}, u32[]{:S(2)}) copy-start(bf16[256,1024]{1,0:T(8,128)(2,1)} %get-tuple-element.32) | copy-start | bytes 1572868
  285.3 2.2 copy-start.7
  285.3 3.0 %copy-start.6 = (bf16[256,1024]{1,0:T(8,128)(2,1)S(1)}, bf16[256,1024]{1,0:T(8,128)(2,1)}, u32[]{:S(2)}) copy-start(bf16[256,1024]{1,0:T(8,128)(2,1)} %get-tuple-element.56) | copy-start | bytes 1572868
  286.4 2.7 copy-start.5
